TPU v7x, 1024 devices: a whole 8x8x8 slice. The times are simulated.
1024 devices in a mesh: seq: 16 (over z, core), col: 8 (over y), row: 8 (over x).
Axes of the slice: x: 8, y: 8, z: 8, core: 2. Of those that a mesh axis runs over, the one named last changes fastest.
Arguments:
- table: bfloat16 [32768, 2048], P('seq', 'col'), may hold values from -6 to 6
- w_qkv: bfloat16 [2048, 3, 2048], P(None, None, 'col')
- gain: float32 [2048], replicated, may hold values from 0.1 to 1.9
- ngram_ids: int32 [8, 2048, 2], P('row', 'seq'), may hold values from 0 to 32767, as said below
- segment_ids: int32 [8, 2048], P('row', 'seq'), may hold values from 0 to 3, never falling along the last dimension, each value on 1 to 1024 neighbouring positions
- d_pooled: bfloat16 [8, 2048, 2048], P('row', 'seq', 'col'), may hold values from -6 to 6
Outputs:
- pooled: bfloat16 [8, 2048, 2048], P('row', 'seq', 'col')
- context: bfloat16 [8, 2048, 2048], P('row', 'seq', 'col')
- table_grad: bfloat16 [32768, 2048], P(('seq', 'row'), 'col')
Inputs may be any that keep to these rules, and one draw needn't show every extreme that they name: `ngram_ids`: the 256 ids of one device's tokens (the 128 positions of one sequence on one index of seq, both n-grams) fall into any one block of 256 consecutive table rows at most 4 times, and exactly 4 times into some block.
All inputs are finite; a program needn't handle non-finite values.
Results may differ from a plain program's by a relative error of at most 0.0092.
Values may be sent and summed in bfloat16 or wider, within the bound.
A program may use at most 32 MiB of HBM per device.

v0:
```python
import math

import jax
import jax.numpy as jnp
from jax import lax
from jax.sharding import PartitionSpec as P

HD = 128


def rotate(values, positions):
    half = values.shape[-1] // 2
    inverse = 10000.0 ** (-(jnp.arange(half, dtype=jnp.float32) * 2.0 / values.shape[-1]))
    angles = positions.astype(jnp.float32)[:, None] * inverse[None, :]
    cosine = jnp.cos(angles)[:, None, :]
    sine = jnp.sin(angles)[:, None, :]
    first = values[..., :half]
    second = values[..., half:]
    return jnp.concatenate(
        [first * cosine - second * sine, second * cosine + first * sine], axis=-1
    )


def local(table, w_qkv, gain, ngram_ids, segment_ids, d_pooled):
    seq_count = lax.axis_size("seq")
    row_count = lax.axis_size("row")
    shard_rows = table.shape[0] // row_count
    columns = table.shape[1]
    tok_count = ngram_ids.shape[1]
    shard_count = seq_count * row_count
    capacity = 4 * tok_count // shard_count
    total_slots = shard_count * capacity
    lookup_ids = ngram_ids.reshape(-1)
    target = lookup_ids // shard_rows
    hits = (target[:, None] == jnp.arange(shard_count, dtype=jnp.int32)[None, :]).astype(jnp.int32)
    earlier = jnp.cumsum(hits, axis=0) - hits
    slot_index = target * capacity + jnp.sum(earlier * hits, axis=1)
    local_rows = lookup_ids % (row_count * shard_rows)
    send_flat = jnp.zeros((total_slots,), jnp.int32).at[slot_index].set(local_rows)
    send_rows = send_flat.reshape(seq_count, row_count * capacity)
    cotangent = jnp.broadcast_to(d_pooled[0][:, None, :], (tok_count, 2, columns)).reshape(
        -1, columns
    )
    grads_flat = jnp.zeros((total_slots, columns), jnp.bfloat16).at[slot_index].set(cotangent)
    send_grads = grads_flat.reshape(seq_count, row_count * capacity, columns)
    wanted = lax.all_to_all(send_rows, "seq", split_axis=0, concat_axis=0, tiled=True)
    grads_in = lax.all_to_all(send_grads, "seq", split_axis=0, concat_axis=0, tiled=True)
    fetched = jnp.take(table, wanted, axis=0)
    returned = lax.all_to_all(fetched, "seq", split_axis=0, concat_axis=0, tiled=True)
    fetched_rows = returned.reshape(total_slots, columns)[slot_index].reshape(tok_count, 2, columns)
    pooled = (
        fetched_rows[:, 0].astype(jnp.float32) + fetched_rows[:, 1].astype(jnp.float32)
    ).astype(jnp.bfloat16)
    features = lax.all_gather(pooled, "col", axis=1, tiled=True)
    wide = features.astype(jnp.float32)
    normed = (
        wide * lax.rsqrt(jnp.mean(wide * wide, axis=-1, keepdims=True) + 1e-05) * gain
    ).astype(jnp.bfloat16)
    heads_here = w_qkv.shape[2] // HD
    positions = lax.axis_index("seq") * tok_count + jnp.arange(tok_count, dtype=jnp.int32)
    mixed = jnp.einsum("td,dch->tch", normed, w_qkv, preferred_element_type=jnp.float32)
    queries = rotate(mixed[:, 0].reshape(tok_count, heads_here, HD), positions).astype(jnp.bfloat16)
    keys_here = rotate(mixed[:, 1].reshape(tok_count, heads_here, HD), positions).astype(
        jnp.bfloat16
    )
    keys_here = keys_here.reshape(tok_count, heads_here * HD)
    values_here = mixed[:, 2].astype(jnp.bfloat16)
    own_segments = segment_ids[0]
    scale = 1.0 / math.sqrt(HD)
    best = jnp.full((heads_here, tok_count), -1e30, jnp.float32)
    key_block = lax.all_gather(keys_here, "seq", axis=0, tiled=True)
    value_block = lax.all_gather(values_here, "seq", axis=0, tiled=True)
    key_segments = lax.all_gather(own_segments, "seq", axis=0, tiled=True)
    count = key_block.shape[0]
    key_positions = jnp.arange(count, dtype=jnp.int32)
    scores = (
        jnp.einsum(
            "thd,shd->hts",
            queries,
            key_block.reshape(count, heads_here, HD),
            preferred_element_type=jnp.float32,
        )
        * scale
    )
    allowed = (key_positions[None, :] <= positions[:, None]) & (
        key_segments[None, :] == own_segments[:, None]
    )
    scores = jnp.where(allowed[None], scores, -1e30)
    updated = jnp.maximum(best, jnp.max(scores, axis=-1))
    weights = jnp.where(allowed[None], jnp.exp(scores - updated[..., None]), 0.0)
    weight_sum = jnp.sum(weights, axis=-1)
    accum = jnp.einsum(
        "hts,shd->htd",
        weights.astype(jnp.bfloat16),
        value_block.reshape(count, heads_here, HD),
        preferred_element_type=jnp.float32,
    )
    best, weight_sum, accum = (updated, weight_sum, accum)
    context = (
        (accum / weight_sum[..., None])
        .transpose(1, 0, 2)
        .reshape(tok_count, heads_here * HD)
        .astype(jnp.bfloat16)
    )
    dense = jnp.zeros((row_count * shard_rows, columns), jnp.float32)
    dense = dense.at[wanted.reshape(-1)].add(grads_in.reshape(-1, columns).astype(jnp.float32))
    table_grad = lax.psum_scatter(
        dense.astype(jnp.bfloat16), "row", scatter_dimension=0, tiled=True
    )
    return (pooled[None], context[None], table_grad)


def solution(mesh):
    placed = (
        P("seq", "col"),
        P(None, None, "col"),
        P(),
        P("row", "seq", None),
        P("row", "seq"),
        P("row", "seq", "col"),
    )
    return jax.shard_map(
        local,
        mesh=mesh,
        in_specs=placed,
        out_specs=(P("row", "seq", "col"), P("row", "seq", "col"), P(("seq", "row"), "col")),
        check_vma=False,
    )
```

profile of v0, /device:TPU:1, one launch (start us, length us, event | category | flops | bytes accessed | tf_op | source)
XLA Modules:
  0.0 185.6 jit_solution(8063609543270953315)
XLA Ops:
  8.0 0.0 copy-start
  8.0 0.9 copy.32
  8.9 0.1 reshape.397
  9.1 0.1 reshape.396
  9.2 0.1 reshape.395
  9.4 0.1 copy.35
  9.5 0.2 fusion.22
  9.8 0.2 fusion.24
  10.0 0.0 copy-start.4
  10.0 1.4 scatter_custom_fusion
  11.4 0.1 all_to_all.16
  11.5 25.0 %all_to_all.25 = s32[16,1,32]{2,1,0:T(1,128)S(1)} all-to-all(s32[16,1,32]{2,1,0:T(1,128)S(1)} %all_to_all.16), channel_id=1, replica_groups=mesh['seq'=16,'col'=8,'row'=8] {'seq'}, dimensions={0} | all-to-all | bytes 4096 | tf_op jit(solution)/shard_map/all_to_all | solution.py:46
  36.5 0.1 reshape.409
  36.6 2.9 %gather_fusion = bf16[512,256]{1,0:T(8,128)(2,1)S(1)} fusion(bf16[2048,256]{1,0:T(8,128)(2,1)} %param.6, s32[1024]{0:T(1024)S(1)} %pad_clamp_fusion.1), kind=kCustom, calls=%fused_computation | custom fusion | bytes 526336 | tf_op jit(solution)/shard_map/jit(_take)/gather | solution.py:48
  39.6 0.8 broadcast_select_fusion
  40.4 4.1 %all-to-all-start.1 = ((bf16[16,32,256]{2,1,0:T(8,128)(2,1)}), bf16[16,32,256]{2,1,0:T(8,128)(2,1)S(1)}, u32[]{:S(2)}, u32[]{:S(2)}) async-start(bf16[16,32,256]{2,1,0:T(8,128)(2,1)} %broadcast_select_fusion), calls=%async_computation.1 | async-start | bytes 524288 | tf_op jit(solution)/shard_map/all_to_all | solution.py:49
  44.5 0.0 all-gather.8.cloned.1.call-start
  44.6 0.6 pad_clamp_fusion
  45.1 11.2 %all-to-all-done.1 = bf16[16,32,256]{2,1,0:T(8,128)(2,1)S(1)} async-done(((bf16[16,32,256]{2,1,0:T(8,128)(2,1)}), bf16[16,32,256]{2,1,0:T(8,128)(2,1)S(1)}, u32[]{:S(2)}, u32[]{:S(2)}) %all-to-all-start.1) | async-done | bytes 262176 | tf_op jit(solution)/shard_map/all_to_all | solution.py:49
  56.4 0.0 copy-done.4
  56.4 1.3 gather_fusion.1
  57.7 0.1 reshape.400
  57.7 0.2 fusion.40
  57.9 0.0 copy-start.2
  58.0 0.6 copy-done.2
  58.6 22.1 %all-gather.1 = bf16[128,1,2048]{2,0,1:T(8,128)(2,1)S(1)} all-gather(bf16[128,1,256]{2,0,1:T(8,128)(2,1)S(1)} %add_convert_fusion.2), channel_id=3, replica_groups=mesh['seq'=16,'col'=8,'row'=8] {'col'}, dimensions={2}, use_global_device_ids=true | all-gather | bytes 589824 | tf_op jit(solution)/shard_map/all_gather | solution.py:54
  80.7 0.2 fusion.5
  80.9 0.0 copy-done
  80.9 0.0 copy-done.3
  80.9 0.6 fusion.16
  81.5 0.6 slice.61
  82.2 0.0 all-gather.8.cloned.1.call-update
  82.2 0.0 all-gather.6.cloned.1.call-start
  82.3 1.0 multiply_cosine_fusion
  83.2 0.7 fusion.37
  83.9 1.0 reshape_squeeze.6
  84.9 1.0 reshape_squeeze.7
  85.9 0.3 fusion.38
  86.2 1.0 subtract_convert_fusion.1
  87.2 0.1 pad_maximum_fusion
  87.3 0.7 copy.43
  88.0 0.0 all-gather.6.cloned.1.call-update
  88.0 0.9 broadcast_in_dim.78
  89.0 0.1 reshape.435
  89.0 2.3 %scatter_custom_fusion.1 = bf16[512,256]{1,0:T(8,128)(2,1)} fusion(s32[256]{0:T(256)} %bitcast.76, bf16[256,256]{1,0:T(8,128)(2,1)S(1)} %reshape.435, bf16[]{:T(256)} %constant.86.clone.1), kind=kCustom, calls=%fused_computation.38 | custom fusion | bytes 262656 | tf_op jit(solution)/shard_map/scatter | solution.py:44
  91.3 8.4 %all-to-all-start.2 = ((bf16[16,32,256]{2,1,0:T(8,128)(2,1)}), bf16[16,32,256]{2,1,0:T(8,128)(2,1)S(1)}, u32[]{:S(2)}, u32[]{:S(2)}) async-start(bf16[16,32,256]{2,1,0:T(8,128)(2,1)} %bitcast.61), calls=%async_computation.2 | async-start | bytes 524288 | tf_op jit(solution)/shard_map/all_to_all | solution.py:47
  99.7 0.0 reduce-scatter.2.cloned.1.call-start
  99.7 0.5 broadcast.295
  100.2 0.7 reduce.3
  100.9 0.1 reshape.403
  101.0 12.1 %all-to-all-done.2 = bf16[16,32,256]{2,1,0:T(8,128)(2,1)S(1)} async-done(((bf16[16,32,256]{2,1,0:T(8,128)(2,1)}), bf16[16,32,256]{2,1,0:T(8,128)(2,1)S(1)}, u32[]{:S(2)}, u32[]{:S(2)}) %all-to-all-start.2) | async-done | bytes 262176 | tf_op jit(solution)/shard_map/all_to_all | solution.py:47
  113.1 4.8 %scatter_custom_fusion.2 = f32[2048,256]{1,0:T(8,128)} fusion(s32[512]{0:T(512)S(1)} %bitcast.78, f32[]{:T(128)} %constant.78.clone.1, bf16[512,256]{1,0:T(8,128)(2,1)S(1)} %bitcast.58), kind=kCustom, calls=%fused_computation.18 | custom fusion | flops 262144 | bytes 2359300 | tf_op jit(solution)/shard_map/scatter-add | solution.py:106
  117.9 2.7 %convert_element_type.113 = bf16[2048,256]{1,0:T(8,128)(2,1)} convert(f32[2048,256]{1,0:T(8,128)} %scatter_custom_fusion.2) | non-fusion elementwise | flops 524288 | bytes 3145728 | tf_op jit(solution)/shard_map/convert_element_type | solution.py:108
  120.6 0.0 reduce-scatter.2.cloned.1.call-update
  120.6 0.0 copy-done.5
  120.6 14.3 %all-gather = s32[1,2048]{1,0:T(1,128)S(1)} all-gather(s32[1,128]{1,0:T(1,128)S(1)} %copy-done.5), channel_id=2, replica_groups=mesh['seq'=16,'col'=8,'row'=8] {'seq'}, dimensions={1}, use_global_device_ids=true | all-gather | bytes 8704 | tf_op jit(solution)/shard_map/all_gather | solution.py:73
  135.0 0.3 fusion.13
  135.3 0.0 all-gather.8.cloned.1.call-done
  135.3 2.3 %copy.48 = bf16[2048,1,256]{0,2,1:T(8,128)(2,1)} copy(bf16[2048,1,256]{2,0,1:T(8,128)(2,1)} %all-gather.8.cloned.1.call-done) | data formatting | bytes 2097152 | tf_op jit(solution)/shard_map/reshape | solution.py:95
  137.6 36.6 %all-gather.6.cloned.1.call-done = bf16[2048,256]{0,1:T(8,128)(2,1)} async-done(((bf16[128,256]{0,1:T(8,128)(2,1)}), bf16[2048,256]{0,1:T(8,128)(2,1)}) %all-gather.6.cloned.1.call-update) | async-done | bytes 1048592 | tf_op jit(solution)/shard_map/all_gather | solution.py:71
  174.2 2.0 %fusion.41 = (f32[2,128]{1,0:T(2,128)S(1)}, f32[2,128,2048]{2,1,0:T(8,128)S(1)}) fusion(bf16[2048,2,128]{0,2,1:T(8,128)(2,1)} %bitcast.62, bf16[128,2,64]{2,0,1:T(8,128)(2,1)S(1)} %get-tuple-element.13, bf16[128,2,64]{2,0,1:T(8,128)(2,1)S(1)} %get-tuple-element.12, pred[128,2048]{1,0:T(8,128)(4,1)S(1)} %fusion.13), kind=kOutput, calls=%fused_computation.90 | convolution fusion | flops 135921408 | bytes 3474432 | tf_op jit(solution)/shard_map/thd,shd->hts/dot_general | solution.py:77
  176.3 0.6 fusion.1
  176.8 0.6 fusion.4
  177.5 0.7 copy.46
  (24 shorter events, 0.2 us)
Async XLA Ops:
  8.0 72.9 %copy-start = (bf16[2048,3,256]{2,0,1:T(8,128)(2,1)S(1)}, bf16[2048,3,256]{2,0,1:T(8,128)(2,1)}, u32[]{:S(2)}) copy-start(bf16[2048,3,256]{2,0,1:T(8,128)(2,1)} %param.7) | copy-start | bytes 9437188
  10.0 46.3 %copy-start.4 = (s32[256,1]{0,1:T(1,128)}, s32[256,1]{0,1:T(1,128)S(1)}, u32[]{:S(2)}) copy-start(s32[256,1]{0,1:T(1,128)S(1)} %compare_select_fusion.3) | copy-start | bytes 3076
  40.4 40.5 %copy-start.3 = (f32[2048]{0:T(1024)S(1)}, f32[2048]{0:T(1024)}, u32[]{:S(2)}) copy-start(f32[2048]{0:T(1024)} %param.8) | copy-start | bytes 24580
  40.4 16.0 %all-to-all-start.1 = ((bf16[16,32,256]{2,1,0:T(8,128)(2,1)}), bf16[16,32,256]{2,1,0:T(8,128)(2,1)S(1)}, u32[]{:S(2)}, u32[]{:S(2)}) async-start(bf16[16,32,256]{2,1,0:T(8,128)(2,1)} %broadcast_select_fusion), calls=%async_computation.1 | async-start | bytes 524288 | tf_op jit(solution)/shard_map/all_to_all | solution.py:49
  44.5 90.8 %all-gather.8.cloned.1.call-start = ((), (), s32[]{:S(2)}) async-start(), calls=%async_computation.6 | async-start | bytes 1114112 | tf_op jit(solution)/shard_map/all_gather | solution.py:72
  57.9 0.6 copy-start.2
  82.2 92.0 %all-gather.6.cloned.1.call-start = ((), (), s32[]{:S(2)}) async-start(), calls=%async_computation.4 | async-start | bytes 1114112 | tf_op jit(solution)/shard_map/all_gather | solution.py:71
  91.3 21.8 %all-to-all-start.2 = ((bf16[16,32,256]{2,1,0:T(8,128)(2,1)}), bf16[16,32,256]{2,1,0:T(8,128)(2,1)S(1)}, u32[]{:S(2)}, u32[]{:S(2)}) async-start(bf16[16,32,256]{2,1,0:T(8,128)(2,1)} %bitcast.61), calls=%async_computation.2 | async-start | bytes 524288 | tf_op jit(solution)/shard_map/all_to_all | solution.py:47
  99.7 78.6 %reduce-scatter.2.cloned.1.call-start = ((), (), s32[]{:S(2)}) async-start(), calls=%async_computation.5 | async-start | bytes 1179648 | tf_op jit(solution)/shard_map/reduce_scatter | solution.py:107
  117.9 2.7 %copy-start.5 = (s32[1,128]{1,0:T(1,128)S(1)}, s32[1,128]{1,0:T(1,128)}, u32[]{:S(2)}) copy-start(s32[1,128]{1,0:T(1,128)} %param.10) | copy-start | bytes 1540
  174.2 2.6 %copy-start.1 = (bf16[2048,1,256]{0,2,1:T(8,128)(2,1)S(1)}, bf16[2048,1,256]{0,2,1:T(8,128)(2,1)}, u32[]{:S(2)}) copy-start(bf16[2048,1,256]{0,2,1:T(8,128)(2,1)} %copy.48) | copy-start | bytes 3145732
Sparse Core Ops, SparseCore 0:
  82.3 47.2 all-gather.7
  132.2 41.9 all-gather.5
Sparse Core Ops, SparseCore 1:
  120.7 32.8 reduce-scatter.1
where the time goes:
time: 186 us
  blocking collectives  61.4 us (33%)
  waiting for transfers between devices  60 us (32%)
  local copies, waits for them, and re-layouts  19.4 us (10%)
  between operations  15.7 us (8%)
  other arithmetic  13.2 us (7%)
  starting transfers between devices  12.6 us (7%)
  matrix products  3.3 us (2%)
    all_gather x1, waiting for transfers between devices, local(): key_block = lax.all_gather(keys_here, 'seq', axis=0, tiled=True)  36.6 us
    all_to_all x1, blocking collectives, local(): lax.all_to_all(send_rows, 'seq', split_axis=0, concat_axis=0, tiled=True)  25 us
    all_gather x1, blocking collectives, local(): features = lax.all_gather(pooled, 'col', axis=1, tiled=True)  22.1 us
    all_gather x1, blocking collectives, local(): key_segments = lax.all_gather(own_segments, 'seq', axis=0, tiled=True)  14.3 us
    all_to_all x1, waiting for transfers between devices, local(): lax.all_to_all(send_grads, 'seq', split_axis=0, concat_axis=0, tiled=True)  12.1 us
    all_to_all x1, waiting for transfers between devices, local(): lax.all_to_all(fetched, 'seq', split_axis=0, concat_axis=0, tiled=True)  11.2 us
    all_to_all x1, starting transfers between devices, local(): lax.all_to_all(send_grads, 'seq', split_axis=0, concat_axis=0, tiled=True)  8.37 us
    scatter-add x1, other arithmetic, local(): dense.at[wanted.reshape(-1)]  4.79 us
  transfers between devices with their start and end apart: 5, of which 3 were waited for; matrix products, arithmetic and copies ran while one was open for 13% of the time, Pallas kernels for 0%

commit v1 on v0

v1 whole, which is shorter than its diff:
```python
import functools
import math

import jax
import jax.numpy as jnp
import numpy as np
from jax import lax
from jax.experimental import pallas as pl
from jax.experimental.pallas import tpu as pltpu
from jax.sharding import PartitionSpec as P

HD = 128
EPS = 1e-05
WINDOW = 1024
MESH = pl.DeviceIdType.MESH
BF16 = jnp.bfloat16
F32 = jnp.float32
I32 = jnp.int32


def iota(shape, axis):
    return lax.broadcasted_iota(I32, shape, axis)


def hot(mask):
    return jnp.where(mask, 1.0, 0.0).astype(BF16)


def dot(a, b):
    return jnp.dot(a, b, preferred_element_type=F32)


def dot_nt(a, b):
    return lax.dot_general(a, b, (((1,), (1,)), ((), ())), preferred_element_type=F32)


def dot_tn(a, b):
    return lax.dot_general(a, b, (((0,), (0,)), ((), ())), preferred_element_type=F32)


def wait_bytes(ref, sem):
    pltpu.make_async_copy(ref, ref, sem).wait()


def send(src, dst, send_sem, recv_sem, axis, target):
    pltpu.make_async_remote_copy(
        src_ref=src,
        dst_ref=dst,
        send_sem=send_sem,
        recv_sem=recv_sem,
        device_id={axis: target},
        device_id_type=MESH,
    ).start()


def kernel(
    sizes,
    ids_ref,
    seg_ref,
    gain_ref,
    table_hbm,
    w_hbm,
    grad_hbm,
    near_hbm,
    far_hbm,
    pooled_out,
    context_out,
    grad_out,
    table,
    w,
    cot,
    near,
    far,
    req,
    reqs,
    rows_out,
    rows_in,
    gz_out,
    gz_in,
    gx_out,
    gx_in,
    x,
    acc,
    kv,
    ks,
    ctx,
    tg,
    load_sem,
    out_sem,
    req_sem,
    rows_sem,
    gz_sem,
    gx_sem,
    x_send,
    x_recv,
    kv_send,
    kv_recv,
    ks_send,
    ks_recv,
):
    n_seq, n_col, n_row, cap, tok, cols, block = sizes
    own = n_row * cap
    share = n_seq * cap
    slots = n_seq * own
    depth = n_row * block
    heads = cols // HD
    lane_owners = 128 // own
    hops = WINDOW // (2 * tok)

    s = lax.axis_index("seq")
    c = lax.axis_index("col")
    r = lax.axis_index("row")
    core = lax.rem(s, 2)

    loads = [
        pltpu.make_async_copy(src, dst, load_sem.at[i])
        for i, (src, dst) in enumerate(
            ((grad_hbm, cot), (table_hbm, table), (near_hbm, near), (far_hbm, far), (w_hbm, w))
        )
    ]
    for load in loads:
        load.start()

    barrier = pltpu.get_barrier_semaphore()

    def greet(axis, me, count):
        def body(d, carry):
            pl.semaphore_signal(
                barrier, inc=1, device_id={axis: lax.rem(me + d, count)}, device_id_type=MESH
            )
            return carry

        lax.fori_loop(1, count, body, 0)

    greet("seq", s, n_seq)
    greet("row", r, n_row)
    up = lax.rem(c + 1, n_col)
    down = lax.rem(c + n_col - 1, n_col)
    for neighbour in (up, down):
        pl.semaphore_signal(barrier, inc=1, device_id={"col": neighbour}, device_id_type=MESH)

    eye = iota((tok, tok), 0) == iota((tok, tok), 1)
    earlier = iota((tok, tok), 1) < iota((tok, tok), 0)

    def column(row):
        return jnp.sum(jnp.where(eye, row, 0), axis=1, keepdims=True)

    def as_row(col):
        return jnp.sum(jnp.where(eye, col, 0), axis=0, keepdims=True)

    shift = block.bit_length() - 1
    row0, row1 = ids_ref[0:1, :], ids_ref[1:2, :]
    col0, col1 = column(row0), column(row1)
    b0, b1 = jnp.right_shift(row0, shift), jnp.right_shift(row1, shift)
    c0, c1 = jnp.right_shift(col0, shift), jnp.right_shift(col1, shift)

    def count(mask):
        return jnp.sum(jnp.where(mask, 1, 0), axis=1, keepdims=True)

    slot0 = c0 * cap + count((c0 == b0) & earlier)
    slot1 = c1 * cap + count((c1 == b0)) + count((c1 == b1) & earlier)
    lanes = iota((tok, slots), 1)
    hit0, hit1 = slot0 == lanes, slot1 == lanes
    pick = hot(hit0 | hit1)
    local0 = jnp.bitwise_and(col0, depth - 1) + 1
    local1 = jnp.bitwise_and(col1, depth - 1) + 1
    wanted = jnp.sum(jnp.where(hit0, local0, 0) + jnp.where(hit1, local1, 0), axis=0, keepdims=True)
    for g in range(slots // 128):
        req[g : g + 1, :] = wanted[:, 128 * g : 128 * (g + 1)]
    seg_row = seg_ref[...]
    req[slots // 128 : slots // 128 + 1, :] = seg_row
    seg_col = column(seg_row)
    reqs[s] = req[...]
    sub = iota((slots, tok), 0)
    pick_t = hot((as_row(slot0) == sub) | (as_row(slot1) == sub))

    pl.semaphore_wait(barrier, (n_seq - 1) + (n_row - 1) + 2)

    def ask(d, carry):
        send(req, reqs.at[s], req_sem.at[0], req_sem.at[1], "seq", lax.rem(s + d, n_seq))
        return carry

    lax.fori_loop(1, n_seq, ask, 0)

    loads[0].wait()
    gz_out[...] = dot(pick_t, cot[...]).astype(BF16)
    loads[2].wait()
    loads[3].wait()
    near_cos, near_sin = near[0], near[1]
    far_cos, far_sin = far[0, pl.ds(s, 1), :], far[1, pl.ds(s, 1), :]
    cosine = far_cos * near_cos - far_sin * near_sin
    sine = far_sin * near_cos + far_cos * near_sin
    sine = jnp.where(iota((tok, HD), 1) < HD // 2, -sine, sine)
    loads[1].wait()

    wait_bytes(reqs.at[pl.ds(0, n_seq - 1)], req_sem.at[1])
    group = s // lane_owners
    offset = lax.rem(s, lane_owners) * own
    asked = reqs[:, pl.ds(group, 1), :]
    mine = (iota((1, own, 128), 2) - offset) == iota((1, own, 128), 1)
    local = jnp.sum(jnp.where(mine, asked, 0), axis=2, keepdims=True).reshape(slots, 1) - 1
    table_rows = iota((128, depth), 1)
    for g in range(slots // 128):
        found = hot(local[128 * g : 128 * (g + 1)] == table_rows)
        rows_out[128 * g : 128 * (g + 1), :] = dot(found, table[...]).astype(BF16)
        for t in range(g * lane_owners, (g + 1) * lane_owners):

            @pl.when(t != s)
            def _():
                send(
                    rows_out.at[pl.ds(t * own, own)],
                    rows_in.at[pl.ds(pl.multiple_of(s * own, own), own)],
                    rows_sem.at[0],
                    rows_sem.at[1],
                    "seq",
                    t,
                )

    here = pl.ds(pl.multiple_of(s * own, own), own)
    rows_in[here, :] = rows_out[here, :]
    gz_in[here, :] = gz_out[here, :]
    wait_bytes(rows_in.at[pl.ds(0, slots - own)], rows_sem.at[1])
    x[c] = dot(pick, rows_in[...]).astype(BF16)

    half = tok // 2
    full = n_col // 2 - 1

    def piece(j, part):
        return x.at[j, pl.ds(part * half, half)]

    def pass_on(hop, part, way):
        j = lax.rem(c + n_col - hop, n_col) if way == 0 else lax.rem(c + hop, n_col)
        if hop:
            wait_bytes(piece(j, part), x_recv.at[way, hop - 1, part])
        if hop < full or (hop == full and part == way):
            send(
                piece(j, part),
                piece(j, part),
                x_send,
                x_recv.at[way, hop, part],
                "col",
                up if way == 0 else down,
            )

    for part in range(2):
        for way in range(2):
            pass_on(0, part, way)

    pooled_copy = pltpu.make_async_copy(x.at[c], pooled_out, out_sem.at[0])
    pooled_copy.start()

    def give(d, carry):
        t = lax.rem(s + d, n_seq)
        send(
            gz_out.at[pl.ds(pl.multiple_of(t * own, own), own)],
            gz_in.at[pl.ds(pl.multiple_of(s * own, own), own)],
            gz_sem.at[0],
            gz_sem.at[1],
            "seq",
            t,
        )
        return carry

    lax.fori_loop(1, n_seq, give, 0)
    loads[4].wait()

    squares = []

    def project(j, first=False):
        wide = x[j].astype(F32)
        squares.append(jnp.sum(wide * wide, axis=1, keepdims=True))
        scaled = (wide * gain_ref[:, pl.ds(pl.multiple_of(j * cols, cols), cols)]).astype(BF16)
        for i in range(3):
            term = dot(scaled, w[i, j])
            acc[i] = term if first else acc[i] + term

    project(c, True)
    for hop in range(1, full + 1):
        for part in range(2):
            for way in range(2):
                pass_on(hop, part, way)
        project(lax.rem(c + n_col - hop, n_col))
        project(lax.rem(c + hop, n_col))
    for part in range(2):
        pass_on(full + 1, part, part)
    project(lax.rem(c + full + 1, n_col))
    total_square = functools.reduce(jnp.add, squares)
    norm = lax.rsqrt(total_square / (n_col * cols) + EPS)

    def rotated(part):
        return part * cosine + pltpu.roll(part, HD // 2, 1) * sine

    next_chip = lax.rem(s + 2, n_seq)
    sibling = s + 1 - 2 * core

    def kv_send_on(hop, i):
        if hop < hops:
            send(
                kv.at[hop, i],
                kv.at[hop + 1, i],
                kv_send,
                kv_recv.at[hop, i],
                "seq",
                next_chip,
            )

    for i in range(heads):
        part = acc[1, :, HD * i : HD * (i + 1)] * norm
        kv[0, i] = rotated(part).astype(BF16)
        kv_send_on(0, i)
    for i in range(heads):
        kv[0, heads + i] = (acc[2, :, HD * i : HD * (i + 1)] * norm).astype(BF16)
        kv_send_on(0, heads + i)
    queries = [
        rotated(acc[0, :, HD * i : HD * (i + 1)] * norm).astype(BF16) for i in range(heads)
    ]

    wait_bytes(gz_in.at[pl.ds(0, slots - own)], gz_sem.at[1])
    target = iota((slots, slots), 0)
    source_row = target // share
    source_seq = lax.rem(target, share) // cap
    source = source_seq * own + source_row * cap + lax.rem(target, cap)
    moved = hot(source == iota((slots, slots), 1))
    inside = jnp.where(local >= 0, jnp.bitwise_and(local, block - 1), -1)
    beside = jnp.broadcast_to(inside, (slots, 128)).astype(F32).astype(BF16)
    gx_out[:, 0:cols] = dot(moved, gz_in[...]).astype(BF16)
    gx_out[:, cols : cols + 128] = dot(moved, beside).astype(BF16)

    def spread(d, carry):
        t = lax.rem(r + d, n_row)
        send(
            gx_out.at[pl.ds(pl.multiple_of(t * share, share), share)],
            gx_in.at[pl.ds(pl.multiple_of(r * share, share), share)],
            gx_sem.at[0],
            gx_sem.at[1],
            "row",
            t,
        )
        return carry

    lax.fori_loop(1, n_row, spread, 0)
    kept = pl.ds(pl.multiple_of(r * share, share), share)
    gx_in[kept, :] = gx_out[kept, :]

    scale = 1.0 / math.sqrt(HD)
    state = []

    def attend(pieces, first=False):
        masks = []
        for _, back in pieces:
            at = s - back
            keys_seg = reqs[lax.rem(at + n_seq, n_seq), pl.ds(slots // 128, 1), :]
            keys_seg = jnp.where(at >= 0, keys_seg, -1)
            mask = seg_col == keys_seg
            if first:
                mask = mask & (iota((tok, tok), 1) <= iota((tok, tok), 0))
            masks.append(mask)
        for i in range(heads):
            scores = [
                jnp.where(mask, dot_nt(queries[i], ref[i]) * scale, -1e30)
                for (ref, _), mask in zip(pieces, masks)
            ]
            top = functools.reduce(
                jnp.maximum, [jnp.max(score, axis=1, keepdims=True) for score in scores]
            )
            if not first:
                top = jnp.maximum(top, state[i][0])
            weights = [
                jnp.where(mask, jnp.exp(score - top), 0.0) for score, mask in zip(scores, masks)
            ]
            total = functools.reduce(
                jnp.add, [jnp.sum(weight, axis=1, keepdims=True) for weight in weights]
            )
            summed = functools.reduce(
                jnp.add,
                [
                    dot(weight.astype(BF16), ref[heads + i])
                    for (ref, _), weight in zip(pieces, weights)
                ],
            )
            if first:
                state.append((top, total, summed))
            else:
                old_top, old_total, old_summed = state[i]
                fade = jnp.exp(old_top - top)
                state[i] = (top, old_total * fade + total, old_summed * fade + summed)

    attend([(kv.at[0], 0)], True)
    for hop in range(1, hops + 1):
        for i in range(2 * heads):
            wait_bytes(kv.at[hop, i], kv_recv.at[hop - 1, i])
            kv_send_on(hop, i)
        send(
            kv.at[hop - 1 + core],
            ks.at[hop - 1],
            ks_send,
            ks_recv.at[hop - 1],
            "seq",
            sibling,
        )
        pieces = [(kv.at[hop], 2 * hop)]
        if hop > 1:
            wait_bytes(ks.at[hop - 2], ks_recv.at[hop - 2])
            pieces.append((ks.at[hop - 2], 2 * hop - 3))
        attend(pieces)

    wait_bytes(gx_in.at[pl.ds(0, slots - share)], gx_sem.at[1])
    at_row = gx_in[:, cols : cols + 128].astype(F32)
    for g in range(block // 128):
        rows = (iota((slots, 128), 1) + 128 * g).astype(F32)
        tg[128 * g : 128 * (g + 1), :] = dot_tn(hot(at_row == rows), gx_in[:, 0:cols]).astype(BF16)
    tg_copy = pltpu.make_async_copy(tg, grad_out, out_sem.at[1])
    tg_copy.start()

    wait_bytes(ks.at[hops - 1], ks_recv.at[hops - 1])
    attend([(ks.at[hops - 1], 2 * hops - 1)])
    for i in range(heads):
        ctx[:, HD * i : HD * (i + 1)] = (state[i][2] / state[i][1]).astype(BF16)
    ctx_copy = pltpu.make_async_copy(ctx, context_out, out_sem.at[2])
    ctx_copy.start()

    wait_bytes(reqs.at[pl.ds(0, n_seq - 1)], req_sem.at[0])
    wait_bytes(rows_in.at[pl.ds(0, slots - own)], rows_sem.at[0])
    wait_bytes(gz_in.at[pl.ds(0, slots - own)], gz_sem.at[0])
    wait_bytes(gx_in.at[pl.ds(0, slots - share)], gx_sem.at[0])
    wait_bytes(x.at[pl.ds(0, n_col - 1)], x_send)
    wait_bytes(kv.at[pl.ds(0, hops)], kv_send)
    wait_bytes(ks, ks_send)
    pooled_copy.wait()
    tg_copy.wait()
    ctx_copy.wait()


def angle_tables(tok, n_seq):
    inverse = 10000.0 ** (-(np.arange(HD // 2, dtype=np.float64) * 2.0 / HD))
    inverse = np.concatenate([inverse, inverse])
    near = np.arange(tok)[:, None] * inverse[None, :]
    far = (np.arange(n_seq) * tok)[:, None] * inverse[None, :]
    return (
        np.stack([np.cos(near), np.sin(near)]).astype(np.float32),
        np.stack([np.cos(far), np.sin(far)]).astype(np.float32),
    )


def local(n_seq, n_col, n_row, table, w_qkv, gain, ngram_ids, segment_ids, d_pooled):
    depth, cols = table.shape
    tok = ngram_ids.shape[1]
    cap = 4 * tok // (n_seq * n_row)
    block = depth // n_row
    own, share = n_row * cap, n_seq * cap
    slots = n_seq * own
    heads = cols // HD
    hops = WINDOW // (2 * tok)
    near, far = angle_tables(tok, n_seq)
    w = jnp.transpose(w_qkv, (1, 0, 2)).reshape(3, n_col, cols, cols)
    ids = jnp.transpose(ngram_ids[0], (1, 0))
    vmem = pl.BlockSpec(memory_space=pltpu.VMEM)
    anywhere = pl.BlockSpec(memory_space=pltpu.HBM)
    dma = pltpu.SemaphoreType.DMA
    pooled, context, table_grad = pl.pallas_call(
        functools.partial(kernel, (n_seq, n_col, n_row, cap, tok, cols, block)),
        out_shape=(
            jax.ShapeDtypeStruct((tok, cols), BF16),
            jax.ShapeDtypeStruct((tok, cols), BF16),
            jax.ShapeDtypeStruct((block, cols), BF16),
        ),
        in_specs=[vmem] * 3 + [anywhere] * 5,
        out_specs=(anywhere, anywhere, anywhere),
        scratch_shapes=[
            pltpu.VMEM((depth, cols), BF16),
            pltpu.VMEM((3, n_col, cols, cols), BF16),
            pltpu.VMEM((tok, cols), BF16),
            pltpu.VMEM(near.shape, F32),
            pltpu.VMEM(far.shape, F32),
            pltpu.VMEM((8, 128), I32),
            pltpu.VMEM((n_seq, 8, 128), I32),
            pltpu.VMEM((slots, cols), BF16),
            pltpu.VMEM((slots, cols), BF16),
            pltpu.VMEM((slots, cols), BF16),
            pltpu.VMEM((slots, cols), BF16),
            pltpu.VMEM((slots, cols + 128), BF16),
            pltpu.VMEM((slots, cols + 128), BF16),
            pltpu.VMEM((n_col, tok, cols), BF16),
            pltpu.VMEM((3, tok, cols), F32),
            pltpu.VMEM((hops + 1, 2 * heads, tok, HD), BF16),
            pltpu.VMEM((hops, 2 * heads, tok, HD), BF16),
            pltpu.VMEM((tok, cols), BF16),
            pltpu.VMEM((block, cols), BF16),
            dma((5,)),
            dma((3,)),
            dma((2,)),
            dma((2,)),
            dma((2,)),
            dma((2,)),
            dma,
            dma((2, n_col // 2, 2)),
            dma,
            dma((hops, 2 * heads)),
            dma,
            dma((hops,)),
        ],
        compiler_params=pltpu.CompilerParams(
            collective_id=0, has_side_effects=True, vmem_limit_bytes=60 * 1024 * 1024
        ),
        cost_estimate=pl.CostEstimate(
            flops=2 * 10**9, bytes_accessed=5 * 2**20, transcendentals=400000
        ),
    )(
        ids,
        segment_ids,
        gain.reshape(1, -1),
        table,
        w,
        d_pooled[0],
        jnp.asarray(near),
        jnp.asarray(far),
    )
    return pooled[None], context[None], table_grad


def solution(mesh):
    placed = (
        P("seq", "col"),
        P(None, None, "col"),
        P(),
        P("row", "seq", None),
        P("row", "seq"),
        P("row", "seq", "col"),
    )
    n_seq, n_col, n_row = (mesh.shape[axis] for axis in ("seq", "col", "row"))
    return jax.shard_map(
        functools.partial(local, n_seq, n_col, n_row),
        mesh=mesh,
        in_specs=placed,
        out_specs=(P("row", "seq", "col"), P("row", "seq", "col"), P(("seq", "row"), "col")),
        check_vma=False,
    )
```

time: 186 us -> 75 us (0.40)
  Pallas kernels: 0 us -> 69.5 us
  blocking collectives: 61.4 us -> 0 us
  waiting for transfers between devices: 60 us -> 0 us
  between operations: 15.7 us -> 0.64 us
  local copies, waits for them, and re-layouts: 19.4 us -> 4.51 us
  other arithmetic: 13.2 us -> 0 us
  starting transfers between devices: 12.6 us -> 0 us
  matrix products: 3.3 us -> 0 us
    pallas_call x0 -> x1, Pallas kernels: none -> 69.5 us  [local(): pl.pallas_call(functools.partial(kernel, (n_seq, n_col, n_row, cap, tok,...]
    all_gather x2 -> x0, waiting for transfers between devices: 36.6 us -> none  [the longest x1 36.6 us: local(): key_block = lax.all_gather(keys_here, 'seq', axis=0, tiled=True)]
    all_gather x2 -> x0, blocking collectives: 36.4 us -> none  [the longest x1 22.1 us: local(): features = lax.all_gather(pooled, 'col', axis=1, tiled=True)]
    all_to_all x1 -> x0, blocking collectives: 25 us -> none  [local(): lax.all_to_all(send_rows, 'seq', split_axis=0, concat_axis=0, tiled=True)]
    all_to_all x2 -> x0, waiting for transfers between devices: 23.4 us -> none  [the longest x1 12.1 us: local(): lax.all_to_all(send_grads, 'seq', split_axis=0, concat_axis=0, tiled=True)]
    all_to_all x2 -> x0, starting transfers between devices: 12.5 us -> none  [the longest x1 8.37 us: local(): lax.all_to_all(send_grads, 'seq', split_axis=0, concat_axis=0, tiled=True)]
    scatter-add x1 -> x0, other arithmetic: 4.79 us -> none  [local(): dense.at[wanted.reshape(-1)]]
    gather x2 -> x0, local copies, waits for them, and re-layouts: 4.21 us -> none  [the longest x1 2.92 us: local(): fetched = jnp.take(table, wanted, axis=0)]
  transfers between devices with their start and end apart: 5 -> 0, of which waited for: 3 -> 0; matrix products, arithmetic and copies ran while one was open for 13% -> 0% of each run, Pallas kernels for 0% -> 0%
where the time goes in v1:
time: 75 us; the launch traced here: 74.7 us
  Pallas kernels  69.5 us (93%)
  local copies, waits for them, and re-layouts  4.51 us (6%)
    pallas_call x1, Pallas kernels, local(): pl.pallas_call(functools.partial(kernel, (n_seq, n_col, n_row, cap, tok,...  69.5 us
    unnamed x3, local copies, waits for them, and re-layouts  4.51 us

profile of v1, /device:TPU:1, one launch (start us, length us, event | category | flops | bytes accessed | tf_op | source)
XLA Modules:
  0.0 74.7 jit_solution(557867753586144445)
XLA Ops:
  0.6 69.5 %shard_map.103 = (bf16[128,256]{1,0:T(8,128)(2,1)}, bf16[128,256]{1,0:T(8,128)(2,1)}, bf16[256,256]{1,0:T(8,128)(2,1)}) custom-call(s32[2,128]{1,0:T(2,128)} %bitcast.15, s32[1,128]{1,0:T(1,128)} %seg_ref.1, f32[1,2048]{1,0:T(1,128)} %bitcast.14, bf16[2048,256]{1,0:T(8,128)(2,1)} %table_hbm.1, bf16[3,8,256,256]{3,2,1,0:T(8,128)(2,1)} %bitcast.12, ...), custom_call_target="tpu_custom_call" | custom-call | flops 2000000000 | bytes 5242880 | tf_op jit(solution)/shard_map/pallas_call | solution.py:460
  70.2 1.5 %copy.14 = bf16[1,128,256]{2,1,0:T(8,128)(2,1)} copy(bf16[1,128,256]{2,1,0:T(8,128)(2,1)} %bitcast.11) | data formatting | bytes 131072
  71.6 1.5 %copy.15 = bf16[1,128,256]{2,1,0:T(8,128)(2,1)} copy(bf16[1,128,256]{2,1,0:T(8,128)(2,1)} %bitcast.10) | data formatting | bytes 131072
  73.1 1.6 %copy.16 = bf16[256,256]{1,0:T(8,128)(2,1)} copy(bf16[256,256]{1,0:T(8,128)(2,1)} %get-tuple-element.14) | data formatting | bytes 262144

commit v2 on v1

--- a/solution.py
+++ b/solution.py
@@ -12,6 +12,13 @@
 HD = 128
 EPS = 1e-05
 WINDOW = 1024
+
+
+def far_first(count, reach):
+    steps = range(1, count)
+    return sorted(steps, key=lambda d: -min(d // reach, (count - d) // reach))
+
+
 MESH = pl.DeviceIdType.MESH
 BF16 = jnp.bfloat16
 F32 = jnp.float32
@@ -55,9 +62,9 @@
 
 def kernel(
     sizes,
-    ids_ref,
-    seg_ref,
-    gain_ref,
+    ids_hbm,
+    seg_hbm,
+    gain_hbm,
     table_hbm,
     w_hbm,
     grad_hbm,
@@ -66,6 +73,9 @@
     pooled_out,
     context_out,
     grad_out,
+    ids_ref,
+    seg_ref,
+    gain_ref,
     table,
     w,
     cot,
@@ -115,29 +125,41 @@
     loads = [
         pltpu.make_async_copy(src, dst, load_sem.at[i])
         for i, (src, dst) in enumerate(
-            ((grad_hbm, cot), (table_hbm, table), (near_hbm, near), (far_hbm, far), (w_hbm, w))
+            (
+                (ids_hbm, ids_ref),
+                (seg_hbm, seg_ref),
+                (grad_hbm, cot),
+                (table_hbm, table),
+                (near_hbm, near),
+                (far_hbm, far),
+                (gain_hbm, gain_ref),
+                (w_hbm, w),
+            )
         )
     ]
+    got_ids, got_seg, got_cot, got_table, got_near, got_far, got_gain, got_w = loads
     for load in loads:
         load.start()
 
     barrier = pltpu.get_barrier_semaphore()
 
-    def greet(axis, me, count):
-        def body(d, carry):
-            pl.semaphore_signal(
-                barrier, inc=1, device_id={axis: lax.rem(me + d, count)}, device_id_type=MESH
-            )
-            return carry
-
-        lax.fori_loop(1, count, body, 0)
-
-    greet("seq", s, n_seq)
-    greet("row", r, n_row)
-    up = lax.rem(c + 1, n_col)
-    down = lax.rem(c + n_col - 1, n_col)
-    for neighbour in (up, down):
-        pl.semaphore_signal(barrier, inc=1, device_id={"col": neighbour}, device_id_type=MESH)
+    seq_steps = far_first(n_seq, 2)
+
+    def at_seq(step):
+        return lax.rem(s + step, n_seq)
+
+    def at_col(step):
+        return lax.rem(c + (step + n_col), n_col)
+
+    def greet(axis, target):
+        pl.semaphore_signal(barrier, inc=1, device_id={axis: target}, device_id_type=MESH)
+
+    for step in seq_steps:
+        greet("seq", at_seq(step))
+    for step in far_first(n_row, 1):
+        greet("row", lax.rem(r + step, n_row))
+    for step in (-2, -1, 1, 2):
+        greet("col", at_col(step))
 
     eye = iota((tok, tok), 0) == iota((tok, tok), 1)
     earlier = iota((tok, tok), 1) < iota((tok, tok), 0)
@@ -149,6 +171,7 @@
         return jnp.sum(jnp.where(eye, col, 0), axis=0, keepdims=True)
 
     shift = block.bit_length() - 1
+    got_ids.wait()
     row0, row1 = ids_ref[0:1, :], ids_ref[1:2, :]
     col0, col1 = column(row0), column(row1)
     b0, b1 = jnp.right_shift(row0, shift), jnp.right_shift(row1, shift)
@@ -167,6 +190,7 @@
     wanted = jnp.sum(jnp.where(hit0, local0, 0) + jnp.where(hit1, local1, 0), axis=0, keepdims=True)
     for g in range(slots // 128):
         req[g : g + 1, :] = wanted[:, 128 * g : 128 * (g + 1)]
+    got_seg.wait()
     seg_row = seg_ref[...]
     req[slots // 128 : slots // 128 + 1, :] = seg_row
     seg_col = column(seg_row)
@@ -174,146 +198,151 @@
     sub = iota((slots, tok), 0)
     pick_t = hot((as_row(slot0) == sub) | (as_row(slot1) == sub))
 
-    pl.semaphore_wait(barrier, (n_seq - 1) + (n_row - 1) + 2)
-
-    def ask(d, carry):
-        send(req, reqs.at[s], req_sem.at[0], req_sem.at[1], "seq", lax.rem(s + d, n_seq))
-        return carry
-
-    lax.fori_loop(1, n_seq, ask, 0)
-
-    loads[0].wait()
+    pl.semaphore_wait(barrier, (n_seq - 1) + (n_row - 1) + 4)
+    for step in seq_steps:
+        send(req, reqs.at[s], req_sem.at[0], req_sem.at[1], "seq", at_seq(step))
+
+    got_cot.wait()
     gz_out[...] = dot(pick_t, cot[...]).astype(BF16)
-    loads[2].wait()
-    loads[3].wait()
+    got_near.wait()
+    got_far.wait()
     near_cos, near_sin = near[0], near[1]
     far_cos, far_sin = far[0, pl.ds(s, 1), :], far[1, pl.ds(s, 1), :]
     cosine = far_cos * near_cos - far_sin * near_sin
     sine = far_sin * near_cos + far_cos * near_sin
     sine = jnp.where(iota((tok, HD), 1) < HD // 2, -sine, sine)
-    loads[1].wait()
+    got_table.wait()
 
     wait_bytes(reqs.at[pl.ds(0, n_seq - 1)], req_sem.at[1])
     group = s // lane_owners
-    offset = lax.rem(s, lane_owners) * own
-    asked = reqs[:, pl.ds(group, 1), :]
-    mine = (iota((1, own, 128), 2) - offset) == iota((1, own, 128), 1)
-    local = jnp.sum(jnp.where(mine, asked, 0), axis=2, keepdims=True).reshape(slots, 1) - 1
+    groups = slots // 128
+    mine = (iota((1, own, 128), 2) - lax.rem(s, lane_owners) * own) == iota((1, own, 128), 1)
+
+    def asked(first, count):
+        lists = reqs[pl.ds(first, count), pl.ds(group, 1), :]
+        ids = jnp.sum(jnp.where(mine, lists, 0), axis=2, keepdims=True)
+        return ids.reshape(count * own, 1) - 1
+
+    def slots_of(device, count=own):
+        return pl.ds(pl.multiple_of(device * own, own), count)
+
+    here = slots_of(s)
     table_rows = iota((128, depth), 1)
-    for g in range(slots // 128):
-        found = hot(local[128 * g : 128 * (g + 1)] == table_rows)
-        rows_out[128 * g : 128 * (g + 1), :] = dot(found, table[...]).astype(BF16)
-        for t in range(g * lane_owners, (g + 1) * lane_owners):
-
-            @pl.when(t != s)
-            def _():
-                send(
-                    rows_out.at[pl.ds(t * own, own)],
-                    rows_in.at[pl.ds(pl.multiple_of(s * own, own), own)],
-                    rows_sem.at[0],
-                    rows_sem.at[1],
-                    "seq",
-                    t,
-                )
-
-    here = pl.ds(pl.multiple_of(s * own, own), own)
+    for step in [groups // 2] + [i for i in range(1, groups) if i != groups // 2] + [0]:
+        first = lax.rem(group + step, groups) * lane_owners
+        found = hot(asked(first, lane_owners) == table_rows)
+        rows_out[slots_of(first, 128), :] = dot(found, table[...]).astype(BF16)
+        for i in range(lane_owners):
+            if step == 0 and i == 0:
+                continue
+            t = first + (lax.rem(s + i, lane_owners) if step == 0 else i)
+            send(
+                rows_out.at[slots_of(t)],
+                rows_in.at[here],
+                rows_sem.at[0],
+                rows_sem.at[1],
+                "seq",
+                t,
+            )
+
     rows_in[here, :] = rows_out[here, :]
     gz_in[here, :] = gz_out[here, :]
     wait_bytes(rows_in.at[pl.ds(0, slots - own)], rows_sem.at[1])
     x[c] = dot(pick, rows_in[...]).astype(BF16)
 
     half = tok // 2
-    full = n_col // 2 - 1
-
-    def piece(j, part):
-        return x.at[j, pl.ds(part * half, half)]
-
-    def pass_on(hop, part, way):
-        j = lax.rem(c + n_col - hop, n_col) if way == 0 else lax.rem(c + hop, n_col)
-        if hop:
-            wait_bytes(piece(j, part), x_recv.at[way, hop - 1, part])
-        if hop < full or (hop == full and part == way):
-            send(
-                piece(j, part),
-                piece(j, part),
-                x_send,
-                x_recv.at[way, hop, part],
-                "col",
-                up if way == 0 else down,
-            )
-
-    for part in range(2):
+
+    def pass_on(step, way, far, part=None):
+        rows = pl.ds(0, tok) if part is None else pl.ds(part * half, half)
+        piece = x.at[at_col(step), rows]
+        sem = x_recv.at[way, abs(step) + far - 1]
+        send(piece, piece, x_send, sem, "col", at_col(far if way == 0 else -far))
+
+    def arrived(step, way, part=None):
+        rows = pl.ds(0, tok) if part is None else pl.ds(part * half, half)
+        wait_bytes(x.at[at_col(step), rows], x_recv.at[way, abs(step) - 1])
+
+    for far in (2, 1):
         for way in range(2):
-            pass_on(0, part, way)
+            pass_on(0, way, far)
 
     pooled_copy = pltpu.make_async_copy(x.at[c], pooled_out, out_sem.at[0])
     pooled_copy.start()
 
-    def give(d, carry):
-        t = lax.rem(s + d, n_seq)
+    for step in seq_steps:
+        t = at_seq(step)
         send(
-            gz_out.at[pl.ds(pl.multiple_of(t * own, own), own)],
-            gz_in.at[pl.ds(pl.multiple_of(s * own, own), own)],
-            gz_sem.at[0],
-            gz_sem.at[1],
-            "seq",
-            t,
+            gz_out.at[slots_of(t)], gz_in.at[here], gz_sem.at[0], gz_sem.at[1], "seq", t
         )
-        return carry
-
-    lax.fori_loop(1, n_seq, give, 0)
-    loads[4].wait()
+    got_gain.wait()
+    got_w.wait()
 
     squares = []
 
-    def project(j, first=False):
+    def scaled(j):
         wide = x[j].astype(F32)
         squares.append(jnp.sum(wide * wide, axis=1, keepdims=True))
-        scaled = (wide * gain_ref[:, pl.ds(pl.multiple_of(j * cols, cols), cols)]).astype(BF16)
+        return (wide * gain_ref[:, pl.ds(pl.multiple_of(j * cols, cols), cols)]).astype(BF16)
+
+    def project(j, first=False):
+        part = scaled(j)
         for i in range(3):
-            term = dot(scaled, w[i, j])
+            term = dot(part, w[i, j])
             acc[i] = term if first else acc[i] + term
 
     project(c, True)
-    for hop in range(1, full + 1):
-        for part in range(2):
-            for way in range(2):
-                pass_on(hop, part, way)
-        project(lax.rem(c + n_col - hop, n_col))
-        project(lax.rem(c + hop, n_col))
-    for part in range(2):
-        pass_on(full + 1, part, part)
-    project(lax.rem(c + full + 1, n_col))
-    total_square = functools.reduce(jnp.add, squares)
-    norm = lax.rsqrt(total_square / (n_col * cols) + EPS)
+    for way in range(2):
+        step = 2 * way - 1
+        arrived(2 * step, way)
+        pass_on(2 * step, way, 2, way)
+        pass_on(2 * step, way, 1)
+    for distance in (2, 1, 3):
+        for way in range(2):
+            step = distance * (2 * way - 1)
+            if distance != 2:
+                arrived(step, way)
+            project(at_col(step))
+    for way in range(2):
+        arrived(4, way, way)
+    opposite = at_col(4)
+    last = scaled(opposite)
+    norm = lax.rsqrt(functools.reduce(jnp.add, squares) / (n_col * cols) + EPS)
+
+    def projected(i):
+        return (acc[i] + dot(last, w[i, opposite])) * norm
 
     def rotated(part):
-        return part * cosine + pltpu.roll(part, HD // 2, 1) * sine
-
-    next_chip = lax.rem(s + 2, n_seq)
+        return (part * cosine + pltpu.roll(part, HD // 2, 1) * sine).astype(BF16)
+
+    next_chip = at_seq(2)
     sibling = s + 1 - 2 * core
 
-    def kv_send_on(hop, i):
+    def kv_piece(hop, i, part):
+        return kv.at[hop, i, pl.ds(part * half, half)]
+
+    def kv_send_on(hop, i, part):
         if hop < hops:
             send(
-                kv.at[hop, i],
-                kv.at[hop + 1, i],
+                kv_piece(hop, i, part),
+                kv_piece(hop + 1, i, part),
                 kv_send,
-                kv_recv.at[hop, i],
+                kv_recv.at[hop, i, part],
                 "seq",
                 next_chip,
             )
 
+    mixed = projected(1)
     for i in range(heads):
-        part = acc[1, :, HD * i : HD * (i + 1)] * norm
-        kv[0, i] = rotated(part).astype(BF16)
-        kv_send_on(0, i)
+        kv[0, i] = rotated(mixed[:, HD * i : HD * (i + 1)])
+        for part in range(2):
+            kv_send_on(0, i, part)
+    mixed = projected(2)
     for i in range(heads):
-        kv[0, heads + i] = (acc[2, :, HD * i : HD * (i + 1)] * norm).astype(BF16)
-        kv_send_on(0, heads + i)
-    queries = [
-        rotated(acc[0, :, HD * i : HD * (i + 1)] * norm).astype(BF16) for i in range(heads)
-    ]
+        kv[0, heads + i] = mixed[:, HD * i : HD * (i + 1)].astype(BF16)
+        for part in range(2):
+            kv_send_on(0, heads + i, part)
+    mixed = projected(0)
+    queries = [rotated(mixed[:, HD * i : HD * (i + 1)]) for i in range(heads)]
 
     wait_bytes(gz_in.at[pl.ds(0, slots - own)], gz_sem.at[1])
     target = iota((slots, slots), 0)
@@ -321,25 +350,23 @@
     source_seq = lax.rem(target, share) // cap
     source = source_seq * own + source_row * cap + lax.rem(target, cap)
     moved = hot(source == iota((slots, slots), 1))
+    local = asked(0, n_seq)
     inside = jnp.where(local >= 0, jnp.bitwise_and(local, block - 1), -1)
     beside = jnp.broadcast_to(inside, (slots, 128)).astype(F32).astype(BF16)
     gx_out[:, 0:cols] = dot(moved, gz_in[...]).astype(BF16)
     gx_out[:, cols : cols + 128] = dot(moved, beside).astype(BF16)
 
-    def spread(d, carry):
-        t = lax.rem(r + d, n_row)
+    kept = pl.ds(pl.multiple_of(r * share, share), share)
+    for step in far_first(n_row, 1):
+        t = lax.rem(r + step, n_row)
         send(
             gx_out.at[pl.ds(pl.multiple_of(t * share, share), share)],
-            gx_in.at[pl.ds(pl.multiple_of(r * share, share), share)],
+            gx_in.at[kept],
             gx_sem.at[0],
             gx_sem.at[1],
             "row",
             t,
         )
-        return carry
-
-    lax.fori_loop(1, n_row, spread, 0)
-    kept = pl.ds(pl.multiple_of(r * share, share), share)
     gx_in[kept, :] = gx_out[kept, :]
 
     scale = 1.0 / math.sqrt(HD)
@@ -388,8 +415,9 @@
     attend([(kv.at[0], 0)], True)
     for hop in range(1, hops + 1):
         for i in range(2 * heads):
-            wait_bytes(kv.at[hop, i], kv_recv.at[hop - 1, i])
-            kv_send_on(hop, i)
+            for part in range(2):
+                wait_bytes(kv_piece(hop, i, part), kv_recv.at[hop - 1, i, part])
+                kv_send_on(hop, i, part)
         send(
             kv.at[hop - 1 + core],
             ks.at[hop - 1],
@@ -454,19 +482,22 @@
     near, far = angle_tables(tok, n_seq)
     w = jnp.transpose(w_qkv, (1, 0, 2)).reshape(3, n_col, cols, cols)
     ids = jnp.transpose(ngram_ids[0], (1, 0))
-    vmem = pl.BlockSpec(memory_space=pltpu.VMEM)
-    anywhere = pl.BlockSpec(memory_space=pltpu.HBM)
+    hbm = pl.BlockSpec(memory_space=pltpu.HBM)
+    anywhere = pl.BlockSpec(memory_space=pl.ANY)
     dma = pltpu.SemaphoreType.DMA
     pooled, context, table_grad = pl.pallas_call(
         functools.partial(kernel, (n_seq, n_col, n_row, cap, tok, cols, block)),
         out_shape=(
-            jax.ShapeDtypeStruct((tok, cols), BF16),
-            jax.ShapeDtypeStruct((tok, cols), BF16),
-            jax.ShapeDtypeStruct((block, cols), BF16),
+            pltpu.VMEM((tok, cols), BF16),
+            pltpu.VMEM((tok, cols), BF16),
+            pltpu.VMEM((block, cols), BF16),
         ),
-        in_specs=[vmem] * 3 + [anywhere] * 5,
+        in_specs=[hbm] * 8,
         out_specs=(anywhere, anywhere, anywhere),
         scratch_shapes=[
+            pltpu.VMEM(ids.shape, I32),
+            pltpu.VMEM(segment_ids.shape, I32),
+            pltpu.VMEM((1, n_col * cols), F32),
             pltpu.VMEM((depth, cols), BF16),
             pltpu.VMEM((3, n_col, cols, cols), BF16),
             pltpu.VMEM((tok, cols), BF16),
@@ -486,16 +517,16 @@
             pltpu.VMEM((hops, 2 * heads, tok, HD), BF16),
             pltpu.VMEM((tok, cols), BF16),
             pltpu.VMEM((block, cols), BF16),
-            dma((5,)),
+            dma((8,)),
             dma((3,)),
             dma((2,)),
             dma((2,)),
             dma((2,)),
             dma((2,)),
             dma,
-            dma((2, n_col // 2, 2)),
+            dma((2, 4)),
             dma,
-            dma((hops, 2 * heads)),
+            dma((hops, 2 * heads, 2)),
             dma,
             dma((hops,)),
         ],
@@ -515,7 +546,27 @@
         jnp.asarray(near),
         jnp.asarray(far),
     )
+    pooled, context, table_grad = pl.pallas_call(
+        deliver,
+        out_shape=tuple(
+            jax.ShapeDtypeStruct(array.shape, BF16) for array in (pooled, context, table_grad)
+        ),
+        in_specs=[anywhere] * 3,
+        out_specs=(anywhere, anywhere, anywhere),
+        scratch_shapes=[dma((3,))],
+        compiler_params=pltpu.CompilerParams(vmem_limit_bytes=2 * 1024 * 1024),
+        cost_estimate=pl.CostEstimate(flops=0, bytes_accessed=2**19, transcendentals=0),
+    )(pooled, context, table_grad)
     return pooled[None], context[None], table_grad
+
+
+def deliver(pooled, context, grad, pooled_out, context_out, grad_out, sems):
+    pairs = ((pooled, pooled_out), (context, context_out), (grad, grad_out))
+    copies = [pltpu.make_async_copy(*pair, sems.at[i]) for i, pair in enumerate(pairs)]
+    for copy in copies:
+        copy.start()
+    for copy in copies:
+        copy.wait()
 
 
 def solution(mesh):

time: 75 us -> 66.5 us (0.89)
  local copies, waits for them, and re-layouts: 4.51 us -> 0 us
  Pallas kernels: 69.5 us -> 65.7 us
    pallas_call x1, Pallas kernels: 69.5 us -> 65 us  [local(): pl.pallas_call(functools.partial(kernel, (n_seq, n_col, n_row, cap, tok,...]
    unnamed x3 -> x0, local copies, waits for them, and re-layouts: 4.51 us -> none
where the time goes in v2:
time: 66.5 us; the launch traced here: 66.3 us
  Pallas kernels  65.7 us (99%)
    pallas_call x1, Pallas kernels, local(): pl.pallas_call(functools.partial(kernel, (n_seq, n_col, n_row, cap, tok,...  65 us

profile of v2, /device:TPU:1, one launch (start us, length us, event | category | flops | bytes accessed | tf_op | source)
XLA Modules:
  0.0 66.3 jit_solution(2693716812593913227)
XLA Ops:
  0.6 65.0 %shard_map.103 = (bf16[128,256]{1,0:T(8,128)(2,1)S(1)}, bf16[128,256]{1,0:T(8,128)(2,1)S(1)}, bf16[256,256]{1,0:T(8,128)(2,1)S(1)}) custom-call(s32[2,128]{1,0:T(2,128)} %bitcast.15, s32[1,128]{1,0:T(1,128)} %seg_hbm.1, f32[1,2048]{1,0:T(1,128)} %bitcast.14, bf16[2048,256]{1,0:T(8,128)(2,1)} %table_hbm.1, bf16[3,8,256,256]{3,2,1,0:T(8,128)(2,1)} %bitcast.10, ...), custom_call_target="tpu_custom_call" | custom-call | flops 2000000000 | bytes 5242880 | tf_op jit(solution)/shard_map/pallas_call | solution.py:488
  65.6 0.7 %shard_map.104 = (bf16[128,256]{1,0:T(8,128)(2,1)}, bf16[128,256]{1,0:T(8,128)(2,1)}, bf16[256,256]{1,0:T(8,128)(2,1)}) custom-call(bf16[128,256]{1,0:T(8,128)(2,1)S(1)} %get-tuple-element.9.pooled, bf16[128,256]{1,0:T(8,128)(2,1)S(1)} %get-tuple-element.10.context, bf16[256,256]{1,0:T(8,128)(2,1)S(1)} %get-tuple-element.11.grad), custom_call_target="tpu_custom_call" | custom-call | bytes 524288 | tf_op jit(solution)/shard_map/pallas_call | solution.py:549

commit v3 on v2

--- a/solution.py
+++ b/solution.py
@@ -93,6 +93,9 @@
     acc,
     kv,
     ks,
+    tops,
+    totals,
+    sums,
     ctx,
     tg,
     load_sem,
@@ -198,12 +201,23 @@
     sub = iota((slots, tok), 0)
     pick_t = hot((as_row(slot0) == sub) | (as_row(slot1) == sub))
 
+    got_cot.wait()
+    gz_out[...] = dot(pick_t, cot[...]).astype(BF16)
+
+    def slots_of(device, count=own):
+        return pl.ds(pl.multiple_of(device * own, own), count)
+
+    here = slots_of(s)
+
     pl.semaphore_wait(barrier, (n_seq - 1) + (n_row - 1) + 4)
     for step in seq_steps:
         send(req, reqs.at[s], req_sem.at[0], req_sem.at[1], "seq", at_seq(step))
 
-    got_cot.wait()
-    gz_out[...] = dot(pick_t, cot[...]).astype(BF16)
+    for step in seq_steps:
+        t = at_seq(step)
+        send(gz_out.at[slots_of(t)], gz_in.at[here], gz_sem.at[0], gz_sem.at[1], "seq", t)
+    gz_in[here, :] = gz_out[here, :]
+
     got_near.wait()
     got_far.wait()
     near_cos, near_sin = near[0], near[1]
@@ -223,10 +237,6 @@
         ids = jnp.sum(jnp.where(mine, lists, 0), axis=2, keepdims=True)
         return ids.reshape(count * own, 1) - 1
 
-    def slots_of(device, count=own):
-        return pl.ds(pl.multiple_of(device * own, own), count)
-
-    here = slots_of(s)
     table_rows = iota((128, depth), 1)
     for step in [groups // 2] + [i for i in range(1, groups) if i != groups // 2] + [0]:
         first = lax.rem(group + step, groups) * lane_owners
@@ -246,7 +256,32 @@
             )
 
     rows_in[here, :] = rows_out[here, :]
-    gz_in[here, :] = gz_out[here, :]
+
+    wait_bytes(gz_in.at[pl.ds(0, slots - own)], gz_sem.at[1])
+    target = iota((slots, slots), 0)
+    source_row = target // share
+    source_seq = lax.rem(target, share) // cap
+    source = source_seq * own + source_row * cap + lax.rem(target, cap)
+    moved = hot(source == iota((slots, slots), 1))
+    local = asked(0, n_seq)
+    inside = jnp.where(local >= 0, jnp.bitwise_and(local, block - 1), -1)
+    beside = jnp.broadcast_to(inside, (slots, 128)).astype(F32).astype(BF16)
+    gx_out[:, 0:cols] = dot(moved, gz_in[...]).astype(BF16)
+    gx_out[:, cols : cols + 128] = dot(moved, beside).astype(BF16)
+
+    kept = pl.ds(pl.multiple_of(r * share, share), share)
+    for step in far_first(n_row, 1):
+        t = lax.rem(r + step, n_row)
+        send(
+            gx_out.at[pl.ds(pl.multiple_of(t * share, share), share)],
+            gx_in.at[kept],
+            gx_sem.at[0],
+            gx_sem.at[1],
+            "row",
+            t,
+        )
+    gx_in[kept, :] = gx_out[kept, :]
+
     wait_bytes(rows_in.at[pl.ds(0, slots - own)], rows_sem.at[1])
     x[c] = dot(pick, rows_in[...]).astype(BF16)
 
@@ -269,11 +304,6 @@
     pooled_copy = pltpu.make_async_copy(x.at[c], pooled_out, out_sem.at[0])
     pooled_copy.start()
 
-    for step in seq_steps:
-        t = at_seq(step)
-        send(
-            gz_out.at[slots_of(t)], gz_in.at[here], gz_sem.at[0], gz_sem.at[1], "seq", t
-        )
     got_gain.wait()
     got_w.wait()
 
@@ -302,6 +332,14 @@
             if distance != 2:
                 arrived(step, way)
             project(at_col(step))
+    wait_bytes(gx_in.at[pl.ds(0, slots - share)], gx_sem.at[1])
+    at_row = gx_in[:, cols : cols + 128].astype(F32)
+    for g in range(block // 128):
+        rows = (iota((slots, 128), 1) + 128 * g).astype(F32)
+        tg[128 * g : 128 * (g + 1), :] = dot_tn(hot(at_row == rows), gx_in[:, 0:cols]).astype(BF16)
+    tg_copy = pltpu.make_async_copy(tg, grad_out, out_sem.at[1])
+    tg_copy.start()
+
     for way in range(2):
         arrived(4, way, way)
     opposite = at_col(4)
@@ -314,6 +352,7 @@
     def rotated(part):
         return (part * cosine + pltpu.roll(part, HD // 2, 1) * sine).astype(BF16)
 
+    chip = s // 2
     next_chip = at_seq(2)
     sibling = s + 1 - 2 * core
 
@@ -322,13 +361,30 @@
 
     def kv_send_on(hop, i, part):
         if hop < hops:
+
+            @pl.when(chip < n_seq // 2 - 1)
+            def _():
+                send(
+                    kv_piece(hop, i, part),
+                    kv_piece(hop + 1, i, part),
+                    kv_send.at[hop],
+                    kv_recv.at[hop, i, part],
+                    "seq",
+                    next_chip,
+                )
+
+    def share_sends(hop):
+        fits = (hop >= core) & (hop - core < hops) & (chip >= hop)
+
+        @pl.when(fits)
+        def _():
             send(
-                kv_piece(hop, i, part),
-                kv_piece(hop + 1, i, part),
-                kv_send,
-                kv_recv.at[hop, i, part],
+                kv.at[hop],
+                ks.at[hop - core],
+                ks_send.at[hop],
+                ks_recv.at[hop - core],
                 "seq",
-                next_chip,
+                sibling,
             )
 
     mixed = projected(1)
@@ -344,40 +400,12 @@
     mixed = projected(0)
     queries = [rotated(mixed[:, HD * i : HD * (i + 1)]) for i in range(heads)]
 
-    wait_bytes(gz_in.at[pl.ds(0, slots - own)], gz_sem.at[1])
-    target = iota((slots, slots), 0)
-    source_row = target // share
-    source_seq = lax.rem(target, share) // cap
-    source = source_seq * own + source_row * cap + lax.rem(target, cap)
-    moved = hot(source == iota((slots, slots), 1))
-    local = asked(0, n_seq)
-    inside = jnp.where(local >= 0, jnp.bitwise_and(local, block - 1), -1)
-    beside = jnp.broadcast_to(inside, (slots, 128)).astype(F32).astype(BF16)
-    gx_out[:, 0:cols] = dot(moved, gz_in[...]).astype(BF16)
-    gx_out[:, cols : cols + 128] = dot(moved, beside).astype(BF16)
-
-    kept = pl.ds(pl.multiple_of(r * share, share), share)
-    for step in far_first(n_row, 1):
-        t = lax.rem(r + step, n_row)
-        send(
-            gx_out.at[pl.ds(pl.multiple_of(t * share, share), share)],
-            gx_in.at[kept],
-            gx_sem.at[0],
-            gx_sem.at[1],
-            "row",
-            t,
-        )
-    gx_in[kept, :] = gx_out[kept, :]
-
     scale = 1.0 / math.sqrt(HD)
-    state = []
 
     def attend(pieces, first=False):
         masks = []
         for _, back in pieces:
-            at = s - back
-            keys_seg = reqs[lax.rem(at + n_seq, n_seq), pl.ds(slots // 128, 1), :]
-            keys_seg = jnp.where(at >= 0, keys_seg, -1)
+            keys_seg = reqs[lax.rem(s - back + n_seq, n_seq), pl.ds(slots // 128, 1), :]
             mask = seg_col == keys_seg
             if first:
                 mask = mask & (iota((tok, tok), 1) <= iota((tok, tok), 0))
@@ -391,7 +419,8 @@
                 jnp.maximum, [jnp.max(score, axis=1, keepdims=True) for score in scores]
             )
             if not first:
-                top = jnp.maximum(top, state[i][0])
+                old_top = tops[i, :, 0:1]
+                top = jnp.maximum(top, old_top)
             weights = [
                 jnp.where(mask, jnp.exp(score - top), 0.0) for score, mask in zip(scores, masks)
             ]
@@ -405,45 +434,46 @@
                     for (ref, _), weight in zip(pieces, weights)
                 ],
             )
-            if first:
-                state.append((top, total, summed))
-            else:
-                old_top, old_total, old_summed = state[i]
+            if not first:
                 fade = jnp.exp(old_top - top)
-                state[i] = (top, old_total * fade + total, old_summed * fade + summed)
-
+                total = totals[i, :, 0:1] * fade + total
+                summed = sums[i] * fade + summed
+            tops[i] = jnp.broadcast_to(top, (tok, HD))
+            totals[i] = jnp.broadcast_to(total, (tok, HD))
+            sums[i] = summed
+
+    def shared_block(j):
+        wait_bytes(ks.at[j], ks_recv.at[j])
+        return ks.at[j], 2 * j + 1
+
+    share_sends(0)
     attend([(kv.at[0], 0)], True)
     for hop in range(1, hops + 1):
-        for i in range(2 * heads):
-            for part in range(2):
-                wait_bytes(kv_piece(hop, i, part), kv_recv.at[hop - 1, i, part])
-                kv_send_on(hop, i, part)
-        send(
-            kv.at[hop - 1 + core],
-            ks.at[hop - 1],
-            ks_send,
-            ks_recv.at[hop - 1],
-            "seq",
-            sibling,
-        )
-        pieces = [(kv.at[hop], 2 * hop)]
-        if hop > 1:
-            wait_bytes(ks.at[hop - 2], ks_recv.at[hop - 2])
-            pieces.append((ks.at[hop - 2], 2 * hop - 3))
-        attend(pieces)
-
-    wait_bytes(gx_in.at[pl.ds(0, slots - share)], gx_sem.at[1])
-    at_row = gx_in[:, cols : cols + 128].astype(F32)
-    for g in range(block // 128):
-        rows = (iota((slots, 128), 1) + 128 * g).astype(F32)
-        tg[128 * g : 128 * (g + 1), :] = dot_tn(hot(at_row == rows), gx_in[:, 0:cols]).astype(BF16)
-    tg_copy = pltpu.make_async_copy(tg, grad_out, out_sem.at[1])
-    tg_copy.start()
-
-    wait_bytes(ks.at[hops - 1], ks_recv.at[hops - 1])
-    attend([(ks.at[hops - 1], 2 * hops - 1)])
+
+        @pl.when(chip >= hop)
+        def _(hop=hop):
+            for i in range(2 * heads):
+                for part in range(2):
+                    wait_bytes(kv_piece(hop, i, part), kv_recv.at[hop - 1, i, part])
+                    kv_send_on(hop, i, part)
+            share_sends(hop)
+            pieces = [(kv.at[hop], 2 * hop)]
+            if hop > 1:
+                pieces.append(shared_block(hop - 2))
+            attend(pieces)
+
+    reach = jnp.minimum(chip, hops)
+
+    @pl.when(chip >= 1)
+    def _():
+        attend([shared_block(reach - 1)])
+
+    @pl.when((core == 1) & (chip < hops))
+    def _():
+        attend([shared_block(reach)])
+
     for i in range(heads):
-        ctx[:, HD * i : HD * (i + 1)] = (state[i][2] / state[i][1]).astype(BF16)
+        ctx[:, HD * i : HD * (i + 1)] = (sums[i] / totals[i]).astype(BF16)
     ctx_copy = pltpu.make_async_copy(ctx, context_out, out_sem.at[2])
     ctx_copy.start()
 
@@ -452,8 +482,17 @@
     wait_bytes(gz_in.at[pl.ds(0, slots - own)], gz_sem.at[0])
     wait_bytes(gx_in.at[pl.ds(0, slots - share)], gx_sem.at[0])
     wait_bytes(x.at[pl.ds(0, n_col - 1)], x_send)
-    wait_bytes(kv.at[pl.ds(0, hops)], kv_send)
-    wait_bytes(ks, ks_send)
+    for hop in range(hops + 1):
+        if hop < hops:
+
+            @pl.when((chip >= hop) & (chip < n_seq // 2 - 1))
+            def _(hop=hop):
+                wait_bytes(kv.at[hop], kv_send.at[hop])
+
+        @pl.when((hop >= core) & (hop - core < hops) & (chip >= hop))
+        def _(hop=hop):
+            wait_bytes(kv.at[hop], ks_send.at[hop])
+
     pooled_copy.wait()
     tg_copy.wait()
     ctx_copy.wait()
@@ -515,6 +554,9 @@
             pltpu.VMEM((3, tok, cols), F32),
             pltpu.VMEM((hops + 1, 2 * heads, tok, HD), BF16),
             pltpu.VMEM((hops, 2 * heads, tok, HD), BF16),
+            pltpu.VMEM((heads, tok, HD), F32),
+            pltpu.VMEM((heads, tok, HD), F32),
+            pltpu.VMEM((heads, tok, HD), F32),
             pltpu.VMEM((tok, cols), BF16),
             pltpu.VMEM((block, cols), BF16),
             dma((8,)),
@@ -525,9 +567,9 @@
             dma((2,)),
             dma,
             dma((2, 4)),
-            dma,
+            dma((hops,)),
             dma((hops, 2 * heads, 2)),
-            dma,
+            dma((hops + 1,)),
             dma((hops,)),
         ],
         compiler_params=pltpu.CompilerParams(

time: 66.5 us -> 56 us (0.84)
  the two profiles are of different devices: /device:TPU:1 before, /device:TPU:528 now
where the time goes in v3:
time: 56 us; the launch traced here: 55.9 us
  Pallas kernels  55.2 us (99%)
  between operations  0.64 us (1%)
    pallas_call x1, Pallas kernels, local(): pl.pallas_call(functools.partial(kernel, (n_seq, n_col, n_row, cap, tok,...  54.5 us

profile of v3, /device:TPU:528, one launch (start us, length us, event | category | flops | bytes accessed | tf_op | source)
XLA Modules:
  0.0 55.9 jit_solution(8347342872373963513)
XLA Ops:
  0.6 54.5 %shard_map.103 = (bf16[128,256]{1,0:T(8,128)(2,1)S(1)}, bf16[128,256]{1,0:T(8,128)(2,1)S(1)}, bf16[256,256]{1,0:T(8,128)(2,1)S(1)}) custom-call(s32[2,128]{1,0:T(2,128)} %bitcast.15, s32[1,128]{1,0:T(1,128)} %seg_hbm.1, f32[1,2048]{1,0:T(1,128)} %bitcast.14, bf16[2048,256]{1,0:T(8,128)(2,1)} %table_hbm.1, bf16[3,8,256,256]{3,2,1,0:T(8,128)(2,1)} %bitcast.10, ...), custom_call_target="tpu_custom_call" | custom-call | flops 2000000000 | bytes 5242880 | tf_op jit(solution)/shard_map/pallas_call | solution.py:527
  55.1 0.7 %shard_map.104 = (bf16[128,256]{1,0:T(8,128)(2,1)}, bf16[128,256]{1,0:T(8,128)(2,1)}, bf16[256,256]{1,0:T(8,128)(2,1)}) custom-call(bf16[128,256]{1,0:T(8,128)(2,1)S(1)} %get-tuple-element.9.pooled, bf16[128,256]{1,0:T(8,128)(2,1)S(1)} %get-tuple-element.10.context, bf16[256,256]{1,0:T(8,128)(2,1)S(1)} %get-tuple-element.11.grad), custom_call_target="tpu_custom_call" | custom-call | bytes 524288 | tf_op jit(solution)/shard_map/pallas_call | solution.py:591

commit v4 on v3

--- a/solution.py
+++ b/solution.py
@@ -89,6 +89,7 @@
     gz_in,
     gx_out,
     gx_in,
+    moved,
     x,
     acc,
     kv,
@@ -96,11 +97,9 @@
     tops,
     totals,
     sums,
-    ctx,
-    tg,
     load_sem,
-    out_sem,
-    req_sem,
+    req_send,
+    req_recv,
     rows_sem,
     gz_sem,
     gx_sem,
@@ -141,9 +140,6 @@
         )
     ]
     got_ids, got_seg, got_cot, got_table, got_near, got_far, got_gain, got_w = loads
-    for load in loads:
-        load.start()
-
     barrier = pltpu.get_barrier_semaphore()
 
     seq_steps = far_first(n_seq, 2)
@@ -163,6 +159,9 @@
         greet("row", lax.rem(r + step, n_row))
     for step in (-2, -1, 1, 2):
         greet("col", at_col(step))
+
+    for load in loads:
+        load.start()
 
     eye = iota((tok, tok), 0) == iota((tok, tok), 1)
     earlier = iota((tok, tok), 1) < iota((tok, tok), 0)
@@ -198,77 +197,32 @@
     req[slots // 128 : slots // 128 + 1, :] = seg_row
     seg_col = column(seg_row)
     reqs[s] = req[...]
-    sub = iota((slots, tok), 0)
-    pick_t = hot((as_row(slot0) == sub) | (as_row(slot1) == sub))
-
-    got_cot.wait()
-    gz_out[...] = dot(pick_t, cot[...]).astype(BF16)
-
     def slots_of(device, count=own):
         return pl.ds(pl.multiple_of(device * own, own), count)
 
     here = slots_of(s)
 
     pl.semaphore_wait(barrier, (n_seq - 1) + (n_row - 1) + 4)
-    for step in seq_steps:
-        send(req, reqs.at[s], req_sem.at[0], req_sem.at[1], "seq", at_seq(step))
-
-    for step in seq_steps:
-        t = at_seq(step)
-        send(gz_out.at[slots_of(t)], gz_in.at[here], gz_sem.at[0], gz_sem.at[1], "seq", t)
-    gz_in[here, :] = gz_out[here, :]
-
-    got_near.wait()
-    got_far.wait()
-    near_cos, near_sin = near[0], near[1]
-    far_cos, far_sin = far[0, pl.ds(s, 1), :], far[1, pl.ds(s, 1), :]
-    cosine = far_cos * near_cos - far_sin * near_sin
-    sine = far_sin * near_cos + far_cos * near_sin
-    sine = jnp.where(iota((tok, HD), 1) < HD // 2, -sine, sine)
-    got_table.wait()
-
-    wait_bytes(reqs.at[pl.ds(0, n_seq - 1)], req_sem.at[1])
     group = s // lane_owners
     groups = slots // 128
-    mine = (iota((1, own, 128), 2) - lax.rem(s, lane_owners) * own) == iota((1, own, 128), 1)
-
-    def asked(first, count):
-        lists = reqs[pl.ds(first, count), pl.ds(group, 1), :]
-        ids = jnp.sum(jnp.where(mine, lists, 0), axis=2, keepdims=True)
-        return ids.reshape(count * own, 1) - 1
-
-    table_rows = iota((128, depth), 1)
-    for step in [groups // 2] + [i for i in range(1, groups) if i != groups // 2] + [0]:
-        first = lax.rem(group + step, groups) * lane_owners
-        found = hot(asked(first, lane_owners) == table_rows)
-        rows_out[slots_of(first, 128), :] = dot(found, table[...]).astype(BF16)
-        for i in range(lane_owners):
-            if step == 0 and i == 0:
-                continue
-            t = first + (lax.rem(s + i, lane_owners) if step == 0 else i)
-            send(
-                rows_out.at[slots_of(t)],
-                rows_in.at[here],
-                rows_sem.at[0],
-                rows_sem.at[1],
-                "seq",
-                t,
-            )
-
-    rows_in[here, :] = rows_out[here, :]
-
-    wait_bytes(gz_in.at[pl.ds(0, slots - own)], gz_sem.at[1])
-    target = iota((slots, slots), 0)
-    source_row = target // share
-    source_seq = lax.rem(target, share) // cap
-    source = source_seq * own + source_row * cap + lax.rem(target, cap)
-    moved = hot(source == iota((slots, slots), 1))
-    local = asked(0, n_seq)
-    inside = jnp.where(local >= 0, jnp.bitwise_and(local, block - 1), -1)
-    beside = jnp.broadcast_to(inside, (slots, 128)).astype(F32).astype(BF16)
-    gx_out[:, 0:cols] = dot(moved, gz_in[...]).astype(BF16)
-    gx_out[:, cols : cols + 128] = dot(moved, beside).astype(BF16)
-
+    for step in seq_steps:
+        send(req, reqs.at[s], req_send, req_recv.at[group], "seq", at_seq(step))
+
+    def by_row(col, slot):
+        return slot + (col & (n_row - 1)) * (share - cap) + (col >> (n_row.bit_length() - 1)) * (
+            cap - own
+        )
+
+    sub = iota((slots, tok), 0)
+    put0 = as_row(by_row(c0, slot0)) == sub
+    put1 = as_row(by_row(c1, slot1)) == sub
+    inside = jnp.where(put0, (row0 & (block - 1)) + 1, 0) + jnp.where(
+        put1, (row1 & (block - 1)) + 1, 0
+    )
+    inside = jnp.sum(inside, axis=1, keepdims=True) - 1
+    got_cot.wait()
+    gx_out[:, 0:cols] = dot(hot(put0 | put1), cot[...]).astype(BF16)
+    gx_out[:, cols : cols + 128] = jnp.broadcast_to(inside, (slots, 128)).astype(F32).astype(BF16)
     kept = pl.ds(pl.multiple_of(r * share, share), share)
     for step in far_first(n_row, 1):
         t = lax.rem(r + step, n_row)
@@ -282,27 +236,88 @@
         )
     gx_in[kept, :] = gx_out[kept, :]
 
-    wait_bytes(rows_in.at[pl.ds(0, slots - own)], rows_sem.at[1])
-    x[c] = dot(pick, rows_in[...]).astype(BF16)
+    got_near.wait()
+    got_far.wait()
+    near_cos, near_sin = near[0], near[1]
+    far_cos, far_sin = far[0, pl.ds(s, 1), :], far[1, pl.ds(s, 1), :]
+    cosine = far_cos * near_cos - far_sin * near_sin
+    sine = far_sin * near_cos + far_cos * near_sin
+    sine = jnp.where(iota((tok, HD), 1) < HD // 2, -sine, sine)
+    got_table.wait()
+
+    mine = (iota((1, own, 128), 2) - lax.rem(s, lane_owners) * own) == iota((1, own, 128), 1)
+
+    def asked(first, count):
+        lists = reqs[pl.ds(first, count), pl.ds(group, 1), :]
+        ids = jnp.sum(jnp.where(mine, lists, 0), axis=2, keepdims=True)
+        return ids.reshape(count * own, 1) - 1
+
+    halves = cols // 128
+    answers = []
+
+    def answer(t, k):
+        send(
+            rows_out.at[k, slots_of(t)],
+            rows_in.at[k, here],
+            rows_sem.at[0, k],
+            rows_sem.at[1, k],
+            "seq",
+            t,
+        )
+
+    table_rows = iota((128, depth), 1)
+    for step in (0, 1, groups - 1) + tuple(range(2, groups - 1)):
+        theirs = lax.rem(group + step, groups)
+        first = theirs * lane_owners
+        wait_bytes(reqs.at[pl.ds(0, lane_owners - (step == 0))], req_recv.at[theirs])
+        found = hot(asked(first, lane_owners) == table_rows)
+        rows = dot(found, table[...]).astype(BF16)
+        for k in range(halves):
+            rows_out[k, slots_of(first, 128), :] = rows[:, 128 * k : 128 * (k + 1)]
+        for i in range(lane_owners):
+            if step or i:
+                answers.append(first + (i if step else lax.rem(s + i, lane_owners)))
+                answer(answers[-1], 0)
+
+    for k in range(1, halves):
+        for t in answers:
+            answer(t, k)
+
+    rows_in[:, here, :] = rows_out[:, here, :]
+
+    target = iota((slots, slots), 0)
+    source = (lax.rem(target, own) // cap) * share + (target // own) * cap + lax.rem(target, cap)
+    moved[...] = hot(source == iota((slots, slots), 1))
 
     half = tok // 2
 
-    def pass_on(step, way, far, part=None):
+    def piece_of(step, k, part):
         rows = pl.ds(0, tok) if part is None else pl.ds(part * half, half)
-        piece = x.at[at_col(step), rows]
-        sem = x_recv.at[way, abs(step) + far - 1]
-        send(piece, piece, x_send, sem, "col", at_col(far if way == 0 else -far))
-
-    def arrived(step, way, part=None):
-        rows = pl.ds(0, tok) if part is None else pl.ds(part * half, half)
-        wait_bytes(x.at[at_col(step), rows], x_recv.at[way, abs(step) - 1])
-
-    for far in (2, 1):
-        for way in range(2):
-            pass_on(0, way, far)
-
-    pooled_copy = pltpu.make_async_copy(x.at[c], pooled_out, out_sem.at[0])
-    pooled_copy.start()
+        return x.at[k, at_col(step), rows]
+
+    def pass_on(step, way, far, k, part=None):
+        piece = piece_of(step, k, part)
+        sem = x_recv.at[way, abs(step) + far - 1, k]
+        send(piece, piece, x_send.at[k], sem, "col", at_col(far if way == 0 else -far))
+
+    def arrived(step, way, k, part=None):
+        wait_bytes(piece_of(step, k, part), x_recv.at[way, abs(step) - 1, k])
+
+    for k in range(halves):
+        wait_bytes(rows_in.at[k, pl.ds(0, slots - own)], rows_sem.at[1, k])
+        x[k, c] = dot(pick, rows_in[k]).astype(BF16)
+        for far in (2, 1):
+            for way in range(2):
+                pass_on(0, way, far, k)
+
+    for k in range(halves):
+        pooled_out[:, 128 * k : 128 * (k + 1)] = x[k, c]
+    wait_bytes(gx_in.at[pl.ds(0, slots - share)], gx_sem.at[1])
+    gz_out[...] = dot(moved[...], gx_in[...]).astype(BF16)
+    for step in seq_steps:
+        t = at_seq(step)
+        send(gz_out.at[slots_of(t)], gz_in.at[here], gz_sem.at[0], gz_sem.at[1], "seq", t)
+    gz_in[here, :] = gz_out[here, :]
 
     got_gain.wait()
     got_w.wait()
@@ -310,7 +325,7 @@
     squares = []
 
     def scaled(j):
-        wide = x[j].astype(F32)
+        wide = jnp.concatenate([x[k, j] for k in range(halves)], axis=1).astype(F32)
         squares.append(jnp.sum(wide * wide, axis=1, keepdims=True))
         return (wide * gain_ref[:, pl.ds(pl.multiple_of(j * cols, cols), cols)]).astype(BF16)
 
@@ -321,27 +336,22 @@
             acc[i] = term if first else acc[i] + term
 
     project(c, True)
-    for way in range(2):
-        step = 2 * way - 1
-        arrived(2 * step, way)
-        pass_on(2 * step, way, 2, way)
-        pass_on(2 * step, way, 1)
+    for k in range(halves):
+        for way in range(2):
+            step = 2 * way - 1
+            arrived(2 * step, way, k)
+            pass_on(2 * step, way, 2, k, way)
+            pass_on(2 * step, way, 1, k)
     for distance in (2, 1, 3):
         for way in range(2):
             step = distance * (2 * way - 1)
             if distance != 2:
-                arrived(step, way)
+                for k in range(halves):
+                    arrived(step, way, k)
             project(at_col(step))
-    wait_bytes(gx_in.at[pl.ds(0, slots - share)], gx_sem.at[1])
-    at_row = gx_in[:, cols : cols + 128].astype(F32)
-    for g in range(block // 128):
-        rows = (iota((slots, 128), 1) + 128 * g).astype(F32)
-        tg[128 * g : 128 * (g + 1), :] = dot_tn(hot(at_row == rows), gx_in[:, 0:cols]).astype(BF16)
-    tg_copy = pltpu.make_async_copy(tg, grad_out, out_sem.at[1])
-    tg_copy.start()
-
     for way in range(2):
-        arrived(4, way, way)
+        for k in range(halves):
+            arrived(4, way, k, way)
     opposite = at_col(4)
     last = scaled(opposite)
     norm = lax.rsqrt(functools.reduce(jnp.add, squares) / (n_col * cols) + EPS)
@@ -448,6 +458,12 @@
 
     share_sends(0)
     attend([(kv.at[0], 0)], True)
+
+    wait_bytes(gz_in.at[pl.ds(0, slots - own)], gz_sem.at[1])
+    at_row = gz_in[:, cols : cols + 128].astype(F32)
+    for g in range(block // 128):
+        rows = (iota((slots, 128), 1) + 128 * g).astype(F32)
+        grad_out[128 * g : 128 * (g + 1), :] = dot_tn(hot(at_row == rows), gz_in[:, 0:cols]).astype(BF16)
     for hop in range(1, hops + 1):
 
         @pl.when(chip >= hop)
@@ -473,15 +489,13 @@
         attend([shared_block(reach)])
 
     for i in range(heads):
-        ctx[:, HD * i : HD * (i + 1)] = (sums[i] / totals[i]).astype(BF16)
-    ctx_copy = pltpu.make_async_copy(ctx, context_out, out_sem.at[2])
-    ctx_copy.start()
-
-    wait_bytes(reqs.at[pl.ds(0, n_seq - 1)], req_sem.at[0])
-    wait_bytes(rows_in.at[pl.ds(0, slots - own)], rows_sem.at[0])
+        context_out[:, HD * i : HD * (i + 1)] = (sums[i] / totals[i]).astype(BF16)
+    wait_bytes(reqs.at[pl.ds(0, n_seq - 1)], req_send)
+    for k in range(halves):
+        wait_bytes(rows_in.at[k, pl.ds(0, slots - own)], rows_sem.at[0, k])
+        wait_bytes(x.at[k, pl.ds(0, n_col - 1)], x_send.at[k])
     wait_bytes(gz_in.at[pl.ds(0, slots - own)], gz_sem.at[0])
     wait_bytes(gx_in.at[pl.ds(0, slots - share)], gx_sem.at[0])
-    wait_bytes(x.at[pl.ds(0, n_col - 1)], x_send)
     for hop in range(hops + 1):
         if hop < hops:
 
@@ -492,10 +506,6 @@
         @pl.when((hop >= core) & (hop - core < hops) & (chip >= hop))
         def _(hop=hop):
             wait_bytes(kv.at[hop], ks_send.at[hop])
-
-    pooled_copy.wait()
-    tg_copy.wait()
-    ctx_copy.wait()
 
 
 def angle_tables(tok, n_seq):
@@ -522,6 +532,7 @@
     w = jnp.transpose(w_qkv, (1, 0, 2)).reshape(3, n_col, cols, cols)
     ids = jnp.transpose(ngram_ids[0], (1, 0))
     hbm = pl.BlockSpec(memory_space=pltpu.HBM)
+    vmem = pl.BlockSpec(memory_space=pltpu.VMEM)
     anywhere = pl.BlockSpec(memory_space=pl.ANY)
     dma = pltpu.SemaphoreType.DMA
     pooled, context, table_grad = pl.pallas_call(
@@ -532,7 +543,7 @@
             pltpu.VMEM((block, cols), BF16),
         ),
         in_specs=[hbm] * 8,
-        out_specs=(anywhere, anywhere, anywhere),
+        out_specs=(vmem, vmem, vmem),
         scratch_shapes=[
             pltpu.VMEM(ids.shape, I32),
             pltpu.VMEM(segment_ids.shape, I32),
@@ -544,29 +555,28 @@
             pltpu.VMEM(far.shape, F32),
             pltpu.VMEM((8, 128), I32),
             pltpu.VMEM((n_seq, 8, 128), I32),
-            pltpu.VMEM((slots, cols), BF16),
-            pltpu.VMEM((slots, cols), BF16),
-            pltpu.VMEM((slots, cols), BF16),
-            pltpu.VMEM((slots, cols), BF16),
+            pltpu.VMEM((cols // 128, slots, 128), BF16),
+            pltpu.VMEM((cols // 128, slots, 128), BF16),
             pltpu.VMEM((slots, cols + 128), BF16),
             pltpu.VMEM((slots, cols + 128), BF16),
-            pltpu.VMEM((n_col, tok, cols), BF16),
+            pltpu.VMEM((slots, cols + 128), BF16),
+            pltpu.VMEM((slots, cols + 128), BF16),
+            pltpu.VMEM((slots, slots), BF16),
+            pltpu.VMEM((cols // 128, n_col, tok, 128), BF16),
             pltpu.VMEM((3, tok, cols), F32),
             pltpu.VMEM((hops + 1, 2 * heads, tok, HD), BF16),
             pltpu.VMEM((hops, 2 * heads, tok, HD), BF16),
             pltpu.VMEM((heads, tok, HD), F32),
             pltpu.VMEM((heads, tok, HD), F32),
             pltpu.VMEM((heads, tok, HD), F32),
-            pltpu.VMEM((tok, cols), BF16),
-            pltpu.VMEM((block, cols), BF16),
             dma((8,)),
-            dma((3,)),
+            dma,
+            dma((n_seq * own // 128,)),
+            dma((2, cols // 128)),
             dma((2,)),
             dma((2,)),
-            dma((2,)),
-            dma((2,)),
-            dma,
-            dma((2, 4)),
+            dma((cols // 128,)),
+            dma((2, 4, cols // 128)),
             dma((hops,)),
             dma((hops, 2 * heads, 2)),
             dma((hops + 1,)),

time: 56 us -> 52.8 us (0.943)
  the two profiles are of different devices: /device:TPU:528 before, /device:TPU:385 now
where the time goes in v4:
time: 52.8 us; the launch traced here: 52.6 us
  Pallas kernels  52 us (98%)
  between operations  0.64 us (1%)
    pallas_call x1, Pallas kernels, local(): pl.pallas_call(functools.partial(kernel, (n_seq, n_col, n_row, cap, tok,...  51.3 us

profile of v4, /device:TPU:385, one launch (start us, length us, event | category | flops | bytes accessed | tf_op | source)
XLA Modules:
  0.0 52.6 jit_solution(13861303599128348574)
XLA Ops:
  0.6 51.3 %shard_map.103 = (bf16[128,256]{1,0:T(8,128)(2,1)S(1)}, bf16[128,256]{1,0:T(8,128)(2,1)S(1)}, bf16[256,256]{1,0:T(8,128)(2,1)S(1)}) custom-call(s32[2,128]{1,0:T(2,128)} %bitcast.15, s32[1,128]{1,0:T(1,128)} %seg_hbm.1, f32[1,2048]{1,0:T(1,128)} %bitcast.14, bf16[2048,256]{1,0:T(8,128)(2,1)} %table_hbm.1, bf16[3,8,256,256]{3,2,1,0:T(8,128)(2,1)} %bitcast.10, ...), custom_call_target="tpu_custom_call" | custom-call | flops 2000000000 | bytes 5242880 | tf_op jit(solution)/shard_map/pallas_call | solution.py:538
  51.9 0.7 %shard_map.104 = (bf16[128,256]{1,0:T(8,128)(2,1)}, bf16[128,256]{1,0:T(8,128)(2,1)}, bf16[256,256]{1,0:T(8,128)(2,1)}) custom-call(bf16[128,256]{1,0:T(8,128)(2,1)S(1)} %get-tuple-element.9.pooled, bf16[128,256]{1,0:T(8,128)(2,1)S(1)} %get-tuple-element.10.context, bf16[256,256]{1,0:T(8,128)(2,1)S(1)} %get-tuple-element.11.grad), custom_call_target="tpu_custom_call" | custom-call | bytes 524288 | tf_op jit(solution)/shard_map/pallas_call | solution.py:601

commit v5 on v4

--- a/solution.py
+++ b/solution.py
@@ -266,7 +266,7 @@
         )
 
     table_rows = iota((128, depth), 1)
-    for step in (0, 1, groups - 1) + tuple(range(2, groups - 1)):
+    for step in tuple(range(2, groups - 1)) + (1, groups - 1, 0):
         theirs = lax.rem(group + step, groups)
         first = theirs * lane_owners
         wait_bytes(reqs.at[pl.ds(0, lane_owners - (step == 0))], req_recv.at[theirs])
@@ -366,98 +366,97 @@
     next_chip = at_seq(2)
     sibling = s + 1 - 2 * core
 
-    def kv_piece(hop, i, part):
-        return kv.at[hop, i, pl.ds(part * half, half)]
-
-    def kv_send_on(hop, i, part):
+    def kv_piece(hop, i, which, part):
+        return kv.at[hop, i, which, pl.ds(part * half, half)]
+
+    def kv_arrival(hop, i, which, part):
+        return kv_recv.at[hop, i, 2 * which + part]
+
+    def kv_send_on(hop, i, which, part):
         if hop < hops:
 
             @pl.when(chip < n_seq // 2 - 1)
             def _():
                 send(
-                    kv_piece(hop, i, part),
-                    kv_piece(hop + 1, i, part),
+                    kv_piece(hop, i, which, part),
+                    kv_piece(hop + 1, i, which, part),
                     kv_send.at[hop],
-                    kv_recv.at[hop, i, part],
+                    kv_arrival(hop, i, which, part),
                     "seq",
                     next_chip,
                 )
 
-    def share_sends(hop):
+    def share_sends(hop, i):
         fits = (hop >= core) & (hop - core < hops) & (chip >= hop)
 
         @pl.when(fits)
         def _():
             send(
-                kv.at[hop],
-                ks.at[hop - core],
+                kv.at[hop, i],
+                ks.at[hop - core, i],
                 ks_send.at[hop],
-                ks_recv.at[hop - core],
+                ks_recv.at[hop - core, i],
                 "seq",
                 sibling,
             )
 
-    mixed = projected(1)
+    keys = projected(1)
+    values = None
     for i in range(heads):
-        kv[0, i] = rotated(mixed[:, HD * i : HD * (i + 1)])
+        kv[0, i, 0] = rotated(keys[:, HD * i : HD * (i + 1)])
         for part in range(2):
-            kv_send_on(0, i, part)
-    mixed = projected(2)
-    for i in range(heads):
-        kv[0, heads + i] = mixed[:, HD * i : HD * (i + 1)].astype(BF16)
+            kv_send_on(0, i, 0, part)
+        if values is None:
+            values = projected(2)
+        kv[0, i, 1] = values[:, HD * i : HD * (i + 1)].astype(BF16)
         for part in range(2):
-            kv_send_on(0, heads + i, part)
+            kv_send_on(0, i, 1, part)
+        share_sends(0, i)
     mixed = projected(0)
     queries = [rotated(mixed[:, HD * i : HD * (i + 1)]) for i in range(heads)]
 
     scale = 1.0 / math.sqrt(HD)
 
-    def attend(pieces, first=False):
-        masks = []
-        for _, back in pieces:
-            keys_seg = reqs[lax.rem(s - back + n_seq, n_seq), pl.ds(slots // 128, 1), :]
-            mask = seg_col == keys_seg
-            if first:
-                mask = mask & (iota((tok, tok), 1) <= iota((tok, tok), 0))
-            masks.append(mask)
-        for i in range(heads):
-            scores = [
-                jnp.where(mask, dot_nt(queries[i], ref[i]) * scale, -1e30)
-                for (ref, _), mask in zip(pieces, masks)
-            ]
-            top = functools.reduce(
-                jnp.maximum, [jnp.max(score, axis=1, keepdims=True) for score in scores]
-            )
-            if not first:
-                old_top = tops[i, :, 0:1]
-                top = jnp.maximum(top, old_top)
-            weights = [
-                jnp.where(mask, jnp.exp(score - top), 0.0) for score, mask in zip(scores, masks)
-            ]
-            total = functools.reduce(
-                jnp.add, [jnp.sum(weight, axis=1, keepdims=True) for weight in weights]
-            )
-            summed = functools.reduce(
-                jnp.add,
-                [
-                    dot(weight.astype(BF16), ref[heads + i])
-                    for (ref, _), weight in zip(pieces, weights)
-                ],
-            )
-            if not first:
-                fade = jnp.exp(old_top - top)
-                total = totals[i, :, 0:1] * fade + total
-                summed = sums[i] * fade + summed
-            tops[i] = jnp.broadcast_to(top, (tok, HD))
-            totals[i] = jnp.broadcast_to(total, (tok, HD))
-            sums[i] = summed
-
-    def shared_block(j):
-        wait_bytes(ks.at[j], ks_recv.at[j])
-        return ks.at[j], 2 * j + 1
-
-    share_sends(0)
-    attend([(kv.at[0], 0)], True)
+    def mask_of(back):
+        keys_seg = reqs[lax.rem(s - back + n_seq, n_seq), pl.ds(slots // 128, 1), :]
+        return seg_col == keys_seg
+
+    def attend(i, pieces, first=False):
+        scores = [
+            jnp.where(mask, dot_nt(queries[i], ref[0]) * scale, -1e30) for ref, mask in pieces
+        ]
+        top = functools.reduce(
+            jnp.maximum, [jnp.max(score, axis=1, keepdims=True) for score in scores]
+        )
+        if not first:
+            old_top = tops[i, :, 0:1]
+            top = jnp.maximum(top, old_top)
+        weights = [
+            jnp.where(mask, jnp.exp(score - top), 0.0)
+            for score, (_, mask) in zip(scores, pieces)
+        ]
+        total = functools.reduce(
+            jnp.add, [jnp.sum(weight, axis=1, keepdims=True) for weight in weights]
+        )
+        summed = functools.reduce(
+            jnp.add,
+            [dot(weight.astype(BF16), ref[1]) for (ref, _), weight in zip(pieces, weights)],
+        )
+        if not first:
+            fade = jnp.exp(old_top - top)
+            total = totals[i, :, 0:1] * fade + total
+            summed = sums[i] * fade + summed
+        tops[i] = jnp.broadcast_to(top, (tok, HD))
+        totals[i] = jnp.broadcast_to(total, (tok, HD))
+        sums[i] = summed
+
+    def shared(j, i):
+        wait_bytes(ks.at[j, i], ks_recv.at[j, i])
+        return ks.at[j, i]
+
+    causal = mask_of(0) & (iota((tok, tok), 1) <= iota((tok, tok), 0))
+    for i in range(heads):
+        attend(i, [(kv.at[0, i], causal)], True)
 
     wait_bytes(gz_in.at[pl.ds(0, slots - own)], gz_sem.at[1])
     at_row = gz_in[:, cols : cols + 128].astype(F32)
@@ -468,25 +467,34 @@
 
         @pl.when(chip >= hop)
         def _(hop=hop):
-            for i in range(2 * heads):
-                for part in range(2):
-                    wait_bytes(kv_piece(hop, i, part), kv_recv.at[hop - 1, i, part])
-                    kv_send_on(hop, i, part)
-            share_sends(hop)
-            pieces = [(kv.at[hop], 2 * hop)]
-            if hop > 1:
-                pieces.append(shared_block(hop - 2))
-            attend(pieces)
-
-    reach = jnp.minimum(chip, hops)
-
-    @pl.when(chip >= 1)
+            mask = mask_of(2 * hop)
+            j = hop - 2 + core
+            for i in range(heads):
+                for which in range(2):
+                    for part in range(2):
+                        piece = kv_piece(hop, i, which, part)
+                        wait_bytes(piece, kv_arrival(hop - 1, i, which, part))
+                        kv_send_on(hop, i, which, part)
+                share_sends(hop, i)
+                if hop > 1:
+                    attend(i, [(kv.at[hop, i], mask), (shared(j, i), mask_of(2 * j + 1))])
+                else:
+
+                    @pl.when(core == 1)
+                    def _(i=i):
+                        attend(i, [(kv.at[1, i], mask), (shared(0, i), mask_of(1))])
+
+                    @pl.when(core == 0)
+                    def _(i=i):
+                        attend(i, [(kv.at[1, i], mask)])
+
+    rest = jnp.minimum(chip, hops) - 1 + core
+
+    @pl.when((rest >= 0) & (rest < hops))
     def _():
-        attend([shared_block(reach - 1)])
-
-    @pl.when((core == 1) & (chip < hops))
-    def _():
-        attend([shared_block(reach)])
+        mask = mask_of(2 * rest + 1)
+        for i in range(heads):
+            attend(i, [(shared(rest, i), mask)])
 
     for i in range(heads):
         context_out[:, HD * i : HD * (i + 1)] = (sums[i] / totals[i]).astype(BF16)
@@ -564,8 +572,8 @@
             pltpu.VMEM((slots, slots), BF16),
             pltpu.VMEM((cols // 128, n_col, tok, 128), BF16),
             pltpu.VMEM((3, tok, cols), F32),
-            pltpu.VMEM((hops + 1, 2 * heads, tok, HD), BF16),
-            pltpu.VMEM((hops, 2 * heads, tok, HD), BF16),
+            pltpu.VMEM((hops + 1, heads, 2, tok, HD), BF16),
+            pltpu.VMEM((hops, heads, 2, tok, HD), BF16),
             pltpu.VMEM((heads, tok, HD), F32),
             pltpu.VMEM((heads, tok, HD), F32),
             pltpu.VMEM((heads, tok, HD), F32),
@@ -578,9 +586,9 @@
             dma((cols // 128,)),
             dma((2, 4, cols // 128)),
             dma((hops,)),
-            dma((hops, 2 * heads, 2)),
+            dma((hops, heads, 4)),
             dma((hops + 1,)),
-            dma((hops,)),
+            dma((hops, heads)),
         ],
         compiler_params=pltpu.CompilerParams(
             collective_id=0, has_side_effects=True, vmem_limit_bytes=60 * 1024 * 1024

time: 52.8 us -> 52 us (0.985)
  the two profiles are of different devices: /device:TPU:385 before, /device:TPU:512 now
where the time goes in v5:
time: 52 us; the launch traced here: 51.8 us
  Pallas kernels  51.2 us (98%)
  between operations  0.64 us (1%)
    pallas_call x1, Pallas kernels, local(): pl.pallas_call(functools.partial(kernel, (n_seq, n_col, n_row, cap, tok,...  50.5 us

profile of v5, /device:TPU:512, one launch (start us, length us, event | category | flops | bytes accessed | tf_op | source)
XLA Modules:
  0.0 51.8 jit_solution(2069347962268697079)
XLA Ops:
  0.6 50.5 %shard_map.103 = (bf16[128,256]{1,0:T(8,128)(2,1)S(1)}, bf16[128,256]{1,0:T(8,128)(2,1)S(1)}, bf16[256,256]{1,0:T(8,128)(2,1)S(1)}) custom-call(s32[2,128]{1,0:T(2,128)} %bitcast.15, s32[1,128]{1,0:T(1,128)} %seg_hbm.1, f32[1,2048]{1,0:T(1,128)} %bitcast.14, bf16[2048,256]{1,0:T(8,128)(2,1)} %table_hbm.1, bf16[3,8,256,256]{3,2,1,0:T(8,128)(2,1)} %bitcast.10, ...), custom_call_target="tpu_custom_call" | custom-call | flops 2000000000 | bytes 5242880 | tf_op jit(solution)/shard_map/pallas_call | solution.py:546
  51.1 0.7 %shard_map.104 = (bf16[128,256]{1,0:T(8,128)(2,1)}, bf16[128,256]{1,0:T(8,128)(2,1)}, bf16[256,256]{1,0:T(8,128)(2,1)}) custom-call(bf16[128,256]{1,0:T(8,128)(2,1)S(1)} %get-tuple-element.9.pooled, bf16[128,256]{1,0:T(8,128)(2,1)S(1)} %get-tuple-element.10.context, bf16[256,256]{1,0:T(8,128)(2,1)S(1)} %get-tuple-element.11.grad), custom_call_target="tpu_custom_call" | custom-call | bytes 524288 | tf_op jit(solution)/shard_map/pallas_call | solution.py:609

commit v6 on v5

--- a/solution.py
+++ b/solution.py
@@ -458,11 +458,6 @@
     for i in range(heads):
         attend(i, [(kv.at[0, i], causal)], True)
 
-    wait_bytes(gz_in.at[pl.ds(0, slots - own)], gz_sem.at[1])
-    at_row = gz_in[:, cols : cols + 128].astype(F32)
-    for g in range(block // 128):
-        rows = (iota((slots, 128), 1) + 128 * g).astype(F32)
-        grad_out[128 * g : 128 * (g + 1), :] = dot_tn(hot(at_row == rows), gz_in[:, 0:cols]).astype(BF16)
     for hop in range(1, hops + 1):
 
         @pl.when(chip >= hop)
@@ -487,6 +482,13 @@
                     @pl.when(core == 0)
                     def _(i=i):
                         attend(i, [(kv.at[1, i], mask)])
+
+        if hop == 1:
+            wait_bytes(gz_in.at[pl.ds(0, slots - own)], gz_sem.at[1])
+            at_row = gz_in[:, cols : cols + 128].astype(F32)
+            for g in range(block // 128):
+                rows = (iota((slots, 128), 1) + 128 * g).astype(F32)
+                grad_out[128 * g : 128 * (g + 1), :] = dot_tn(hot(at_row == rows), gz_in[:, 0:cols]).astype(BF16)
 
     rest = jnp.minimum(chip, hops) - 1 + core
 

time: 52 us -> 52 us (level)
  no operation moved by 1% of the time
where the time goes in v6:
time: 52 us; the launch traced here: 51.9 us
  Pallas kernels  51.3 us (99%)
  between operations  0.64 us (1%)
    pallas_call x1, Pallas kernels, local(): pl.pallas_call(functools.partial(kernel, (n_seq, n_col, n_row, cap, tok,...  50.5 us

profile of v6, /device:TPU:512, one launch (start us, length us, event | category | flops | bytes accessed | tf_op | source)
XLA Modules:
  0.0 51.9 jit_solution(4950458871921304217)
XLA Ops:
  0.6 50.5 %shard_map.103 = (bf16[128,256]{1,0:T(8,128)(2,1)S(1)}, bf16[128,256]{1,0:T(8,128)(2,1)S(1)}, bf16[256,256]{1,0:T(8,128)(2,1)S(1)}) custom-call(s32[2,128]{1,0:T(2,128)} %bitcast.15, s32[1,128]{1,0:T(1,128)} %seg_hbm.1, f32[1,2048]{1,0:T(1,128)} %bitcast.14, bf16[2048,256]{1,0:T(8,128)(2,1)} %table_hbm.1, bf16[3,8,256,256]{3,2,1,0:T(8,128)(2,1)} %bitcast.10, ...), custom_call_target="tpu_custom_call" | custom-call | flops 2000000000 | bytes 5242880 | tf_op jit(solution)/shard_map/pallas_call | solution.py:548
  51.2 0.7 %shard_map.104 = (bf16[128,256]{1,0:T(8,128)(2,1)}, bf16[128,256]{1,0:T(8,128)(2,1)}, bf16[256,256]{1,0:T(8,128)(2,1)}) custom-call(bf16[128,256]{1,0:T(8,128)(2,1)S(1)} %get-tuple-element.9.pooled, bf16[128,256]{1,0:T(8,128)(2,1)S(1)} %get-tuple-element.10.context, bf16[256,256]{1,0:T(8,128)(2,1)S(1)} %get-tuple-element.11.grad), custom_call_target="tpu_custom_call" | custom-call | bytes 524288 | tf_op jit(solution)/shard_map/pallas_call | solution.py:611
